TPU v7x, 32 devices: a whole 2x2x4 slice. The times are simulated.
32 devices in a mesh: segment: 4 (over x, core), dp: 4 (over z), seq: 2 (over y).
Axes of the slice: x: 2, y: 2, z: 4, core: 2. Of those that a mesh axis runs over, the one named last changes fastest.
Arguments:
- query_in: bfloat16 [16, 256, 1536], P(('segment', 'dp'), 'seq'), may hold values from -6 to 6
- key_in: bfloat16 [16, 256, 1536], P(('segment', 'dp'), 'seq'), may hold values from -6 to 6
- value_in: bfloat16 [16, 256, 1536], P(('segment', 'dp'), 'seq'), may hold values from -6 to 6
- latent_now: bfloat16 [16, 256, 1536], P(('segment', 'dp'), 'seq'), may hold values from -6 to 6
- latent_next: bfloat16 [16, 256, 1536], P(('segment', 'dp'), 'seq'), may hold values from -6 to 6
- norm_gains: float32 [2, 128], replicated, may hold values from 0.1 to 1.9
- rewards: float32 [16], replicated, may hold values from -2 to 2
- step_index: int32 [16], replicated, may hold values from 0 to 15
- token_count: int32 [16], replicated, may hold values from 64 to 256, as said below
Outputs:
- grad_query: bfloat16 [16, 256, 1536], P(('segment', 'dp'), None, 'seq')
- grad_key: bfloat16 [16, 256, 1536], P(('segment', 'dp'), None, 'seq')
- grad_value: bfloat16 [16, 256, 1536], P(('segment', 'dp'), None, 'seq')
- gain_grads: float32 [2, 128], replicated
Inputs may be any that keep to these rules, and one draw needn't show every extreme that they name: `token_count`: valid tokens of each video; some video has exactly 256.
All inputs are finite; a program needn't handle non-finite values.
Results may differ from a plain program's by a relative error of at most 0.018.
Values may be sent and summed in bfloat16 or wider, within the bound.
A program may use at most 64 MiB of HBM per device.

v0:
```python
import jax
import jax.numpy as jnp
from jax import lax
from jax.sharding import PartitionSpec as P

HEAD = 128
STEPS = 16
GROUP = 16


def shifted(value, axis, steps):
    count = lax.axis_size(axis)
    pairs = [(source, (source + steps) % count) for source in range(count)]
    return lax.ppermute(value, axis, pairs)


def head_norm(values, gain):
    wide = values.astype(jnp.float32)
    scaled = wide * lax.rsqrt(jnp.mean(wide * wide, axis=-1, keepdims=True) + 1e-06)
    return (scaled * gain).astype(jnp.bfloat16)


def head_grads(query, keys, values, now_rows, next_rows, gains, advantage, delta, count):
    length = query.shape[0]
    keep = jnp.arange(length) < count

    def forward(q_in, k_in, v_in, gains_in):
        q_rows = head_norm(q_in, gains_in[0])
        k_rows = head_norm(k_in, gains_in[1])
        scores = jnp.dot(q_rows, k_rows.T, preferred_element_type=jnp.float32) / jnp.sqrt(
            jnp.float32(q_in.shape[1])
        )
        scores = jnp.where(keep[None, :], scores, jnp.float32(-1e30))
        weights = jax.nn.softmax(scores, axis=-1).astype(jnp.bfloat16)
        return jnp.dot(weights, v_in, preferred_element_type=jnp.float32)

    velocity, pull = jax.vjp(forward, query, keys, values, gains)
    mean_next = now_rows.astype(jnp.float32) - delta * velocity
    cotangent = jnp.where(
        keep[:, None], advantage * (next_rows.astype(jnp.float32) - mean_next), jnp.float32(0.0)
    )
    return pull(cotangent)


def group_advantage(rewards):
    total = rewards.shape[0]
    member = (jnp.arange(total)[:, None] // GROUP == jnp.arange(total // GROUP)[None, :]).astype(
        jnp.float32
    )
    means = jnp.dot(rewards, member) / GROUP
    mean_rows = jnp.dot(member, means)
    spreads = jnp.sqrt(jnp.dot((rewards - mean_rows) ** 2, member) / GROUP)
    return (rewards - mean_rows) / jnp.maximum(jnp.dot(member, spreads), jnp.float32(0.25))


def step_sigma(index):
    level = 1.0 - index.astype(jnp.float32) / STEPS
    return 7.0 * level / (1.0 + 6.0 * level)


def body(
    query_in,
    key_in,
    value_in,
    latent_now,
    latent_next,
    norm_gains,
    rewards,
    step_index,
    token_count,
):
    segment_count = lax.axis_size("segment")
    replicas = lax.axis_size("dp")
    shards = lax.axis_size("seq")
    source = (lax.axis_index("segment") - 1) % segment_count * replicas + lax.axis_index("dp")
    advantage = group_advantage(rewards)[source]
    delta = (step_sigma(step_index) - step_sigma(step_index + 1))[source]
    count = token_count[source]
    rows = query_in.shape[1]
    head_local = query_in.shape[2] // HEAD // shards
    pieces = tuple(
        (
            a.reshape(rows, shards, head_local, HEAD)
            for a in (query_in, key_in, value_in, latent_now, latent_next)
        )
    )
    arrived = shifted((pieces[0], pieces[1], pieces[2], pieces[3], pieces[4]), "segment", 1)
    items = (
        lax.all_to_all(arrived[0], "seq", split_axis=1, concat_axis=0, tiled=True),
        lax.all_to_all(arrived[1], "seq", split_axis=1, concat_axis=0, tiled=True),
        lax.all_to_all(arrived[2], "seq", split_axis=1, concat_axis=0, tiled=True),
        lax.all_to_all(arrived[3], "seq", split_axis=1, concat_axis=0, tiled=True),
        lax.all_to_all(arrived[4], "seq", split_axis=1, concat_axis=0, tiled=True),
    )
    moved = tuple((jnp.moveaxis(a[:, 0], 1, 0) for a in items))

    def one_head(group):
        return head_grads(
            group[0], group[1], group[2], group[3], group[4], norm_gains, advantage, delta, count
        )

    dq, dk, dv, dg = lax.map(one_head, moved)
    dq, dk, dv, dg = (
        jnp.moveaxis(dq, 0, 1)[:, None],
        jnp.moveaxis(dk, 0, 1)[:, None],
        jnp.moveaxis(dv, 0, 1)[:, None],
        jnp.moveaxis(dg, 0, 1)[:, None],
    )
    gain_total = lax.psum(jnp.sum(dg, axis=(1, 2)), ("segment", "dp", "seq")) / (
        segment_count * replicas
    )
    full_rows = dq.shape[0]
    width = dq.shape[2] * dq.shape[3]
    out_query = dq.reshape(1, full_rows, width)
    out_key = dk.reshape(1, full_rows, width)
    out_value = dv.reshape(1, full_rows, width)
    return (out_query, out_key, out_value, gain_total)


def solution(mesh):
    return jax.shard_map(
        body,
        mesh=mesh,
        in_specs=(
            P(("segment", "dp"), "seq", None),
            P(("segment", "dp"), "seq", None),
            P(("segment", "dp"), "seq", None),
            P(("segment", "dp"), "seq", None),
            P(("segment", "dp"), "seq", None),
            P(),
            P(),
            P(),
            P(),
        ),
        out_specs=(
            P(("segment", "dp"), None, "seq"),
            P(("segment", "dp"), None, "seq"),
            P(("segment", "dp"), None, "seq"),
            P(),
        ),
        check_vma=False,
    )
```

profile of v0, /device:TPU:0, one launch (start us, length us, event | category | flops | bytes accessed | tf_op | source)
XLA Modules:
  0.0 134.7 jit_solution(2771042790419680594)
XLA Ops:
  0.6 1.3 copy.32
  2.7 2.7 %collective-permute-start.1 = (bf16[128,2,6,128]{0,3,2,1:T(8,128)(2,1)S(1)}, bf16[128,2,6,128]{0,3,2,1:T(8,128)(2,1)}, u32[]{:S(2)}, u32[]{:S(2)}) collective-permute-start(bf16[128,2,6,128]{0,3,2,1:T(8,128)(2,1)S(1)} %bitcast.226), channel_id=1, source_target_pairs={{0,8},{8,16},{16,24},{24,0},{1,9},{9,17},{17,25},{25,1},{2,10},{10... | collective-permute-start | bytes 1179656 | tf_op jit(solution)/shard_map/ppermute | solution.py:14
  5.6 4.3 %collective-permute-done = bf16[128,2,6,128]{0,3,2,1:T(8,128)(2,1)} collective-permute-done((bf16[128,2,6,128]{0,3,2,1:T(8,128)(2,1)S(1)}, bf16[128,2,6,128]{0,3,2,1:T(8,128)(2,1)}, u32[]{:S(2)}, u32[]{:S(2)}) %collective-permute-start) | collective-permute-done | bytes 393248 | tf_op jit(solution)/shard_map/ppermute | solution.py:14
  9.9 3.6 %all-to-all-start = ((bf16[128,2,6,128]{0,3,2,1:T(8,128)(2,1)}), bf16[128,2,6,128]{0,3,2,1:T(8,128)(2,1)S(1)}, u32[]{:S(2)}, u32[]{:S(2)}) async-start(bf16[128,2,6,128]{0,3,2,1:T(8,128)(2,1)} %collective-permute-done), calls=%async_computation | async-start | bytes 786432 | tf_op jit(solution)/shard_map/all_to_all | solution.py:93
  14.1 6.1 %all-to-all-done = bf16[128,2,6,128]{0,3,2,1:T(8,128)(2,1)S(1)} async-done(((bf16[128,2,6,128]{0,3,2,1:T(8,128)(2,1)}), bf16[128,2,6,128]{0,3,2,1:T(8,128)(2,1)S(1)}, u32[]{:S(2)}, u32[]{:S(2)}) %all-to-all-start) | async-done | bytes 393248 | tf_op jit(solution)/shard_map/all_to_all | solution.py:93
  20.2 3.5 %all-to-all-start.1 = ((bf16[128,2,6,128]{0,3,2,1:T(8,128)(2,1)}), bf16[128,2,6,128]{0,3,2,1:T(8,128)(2,1)S(1)}, u32[]{:S(2)}, u32[]{:S(2)}) async-start(bf16[128,2,6,128]{0,3,2,1:T(8,128)(2,1)} %collective-permute-done.1), calls=%async_computation.1 | async-start | bytes 786432 | tf_op jit(solution)/shard_map/all_to_all | solution.py:92
  24.0 0.7 copy-done.3
  24.9 0.8 collective-permute-start.2
  25.7 3.8 %all-to-all-done.1 = bf16[128,2,6,128]{0,3,2,1:T(8,128)(2,1)S(1)} async-done(((bf16[128,2,6,128]{0,3,2,1:T(8,128)(2,1)}), bf16[128,2,6,128]{0,3,2,1:T(8,128)(2,1)S(1)}, u32[]{:S(2)}, u32[]{:S(2)}) %all-to-all-start.1) | async-done | bytes 393248 | tf_op jit(solution)/shard_map/all_to_all | solution.py:92
  29.6 3.5 %all-to-all-start.4 = ((bf16[128,2,6,128]{0,3,2,1:T(8,128)(2,1)}), bf16[128,2,6,128]{0,3,2,1:T(8,128)(2,1)S(1)}, u32[]{:S(2)}, u32[]{:S(2)}) async-start(bf16[128,2,6,128]{0,3,2,1:T(8,128)(2,1)} %collective-permute-done.4), calls=%async_computation.4 | async-start | bytes 786432 | tf_op jit(solution)/shard_map/all_to_all | solution.py:91
  35.6 3.3 %all-to-all-done.4 = bf16[128,2,6,128]{0,3,2,1:T(8,128)(2,1)S(1)} async-done(((bf16[128,2,6,128]{0,3,2,1:T(8,128)(2,1)}), bf16[128,2,6,128]{0,3,2,1:T(8,128)(2,1)S(1)}, u32[]{:S(2)}, u32[]{:S(2)}) %all-to-all-start.4) | async-done | bytes 393248 | tf_op jit(solution)/shard_map/all_to_all | solution.py:91
  38.9 3.5 %all-to-all-start.3 = ((bf16[128,2,6,128]{0,3,2,1:T(8,128)(2,1)}), bf16[128,2,6,128]{0,3,2,1:T(8,128)(2,1)S(1)}, u32[]{:S(2)}, u32[]{:S(2)}) async-start(bf16[128,2,6,128]{0,3,2,1:T(8,128)(2,1)} %collective-permute-done.3), calls=%async_computation.3 | async-start | bytes 786432 | tf_op jit(solution)/shard_map/all_to_all | solution.py:90
  42.4 0.7 dynamic_slice.26
  43.6 4.6 %all-to-all-done.3 = bf16[128,2,6,128]{0,3,2,1:T(8,128)(2,1)S(1)} async-done(((bf16[128,2,6,128]{0,3,2,1:T(8,128)(2,1)}), bf16[128,2,6,128]{0,3,2,1:T(8,128)(2,1)S(1)}, u32[]{:S(2)}, u32[]{:S(2)}) %all-to-all-start.3) | async-done | bytes 393248 | tf_op jit(solution)/shard_map/all_to_all | solution.py:90
  48.2 3.5 %all-to-all-start.2 = ((bf16[128,2,6,128]{0,3,2,1:T(8,128)(2,1)}), bf16[128,2,6,128]{0,3,2,1:T(8,128)(2,1)S(1)}, u32[]{:S(2)}, u32[]{:S(2)}) async-start(bf16[128,2,6,128]{0,3,2,1:T(8,128)(2,1)} %collective-permute-done.2), calls=%async_computation.2 | async-start | bytes 786432 | tf_op jit(solution)/shard_map/all_to_all | solution.py:89
  53.3 4.3 %all-to-all-done.2 = bf16[128,2,6,128]{0,3,2,1:T(8,128)(2,1)S(1)} async-done(((bf16[128,2,6,128]{0,3,2,1:T(8,128)(2,1)}), bf16[128,2,6,128]{0,3,2,1:T(8,128)(2,1)S(1)}, u32[]{:S(2)}, u32[]{:S(2)}) %all-to-all-start.2) | async-done | bytes 393248 | tf_op jit(solution)/shard_map/all_to_all | solution.py:89
  57.8 0.7 copy-done.4
  58.6 32.2 %while.16 = (s32[]{:T(128)}, bf16[6,256,128]{1,2,0:T(8,128)(2,1)}, bf16[6,256,128]{1,2,0:T(8,128)(2,1)S(1)}, bf16[6,256,128]{1,2,0:T(8,128)(2,1)S(1)}, f32[6,2,1...) while((s32[]{:T(128)}, bf16[6,256,128]{1,2,0:T(8,128)(2,1)}, ...), condition=%wide.region_10.11_spmd, body=%wide.region_0.10_spmd.sunk | while | flops 104107264 | bytes 5168833 | solution.py:102
  59.8 1.5 %fusion.105 = bf16[256,128]{1,0:T(8,128)(2,1)S(1)} fusion(f32[]{:T(128)} %get-tuple-element.285, bf16[6,256,128]{2,1,0:T(8,128)(2,1)S(1)} %get-tuple-element.284, s32[]{:T(128)S(6)} %copy.73, bf16[6,256,128]{2,1,0:T(8,128)(2,1)S(1)} %get-tuple-element.283, f32[]{:T(128)} %get-tuple-element.282, pred[256]{0:T(512)(128)(4,1)S(1)} %iota_compare_fusion.2, ...), kind=kOutput, calls=%fused_computation.8.clone.1 | convolution fusion | flops 17203200 | bytes 527880 | tf_op jit(solution)/shard_map/while/body/eval_jaxpr/jvp()/dot_general | solution.py:35
  63.9 0.7 iota_compare_fusion.2
  65.2 1.5 %fusion.105 = bf16[256,128]{1,0:T(8,128)(2,1)S(1)} fusion(f32[]{:T(128)} %get-tuple-element.285, bf16[6,256,128]{2,1,0:T(8,128)(2,1)S(1)} %get-tuple-element.284, s32[]{:T(128)S(6)} %copy.73, bf16[6,256,128]{2,1,0:T(8,128)(2,1)S(1)} %get-tuple-element.283, f32[]{:T(128)} %get-tuple-element.282, pred[256]{0:T(512)(128)(4,1)S(1)} %iota_compare_fusion.2, ...), kind=kOutput, calls=%fused_computation.8.clone.1 | convolution fusion | flops 17203200 | bytes 527880 | tf_op jit(solution)/shard_map/while/body/eval_jaxpr/jvp()/dot_general | solution.py:35
  69.3 0.7 iota_compare_fusion.2
  70.5 1.5 %fusion.105 = bf16[256,128]{1,0:T(8,128)(2,1)S(1)} fusion(f32[]{:T(128)} %get-tuple-element.285, bf16[6,256,128]{2,1,0:T(8,128)(2,1)S(1)} %get-tuple-element.284, s32[]{:T(128)S(6)} %copy.73, bf16[6,256,128]{2,1,0:T(8,128)(2,1)S(1)} %get-tuple-element.283, f32[]{:T(128)} %get-tuple-element.282, pred[256]{0:T(512)(128)(4,1)S(1)} %iota_compare_fusion.2, ...), kind=kOutput, calls=%fused_computation.8.clone.1 | convolution fusion | flops 17203200 | bytes 527880 | tf_op jit(solution)/shard_map/while/body/eval_jaxpr/jvp()/dot_general | solution.py:35
  74.7 0.7 iota_compare_fusion.2
  75.9 1.5 %fusion.105 = bf16[256,128]{1,0:T(8,128)(2,1)S(1)} fusion(f32[]{:T(128)} %get-tuple-element.285, bf16[6,256,128]{2,1,0:T(8,128)(2,1)S(1)} %get-tuple-element.284, s32[]{:T(128)S(6)} %copy.73, bf16[6,256,128]{2,1,0:T(8,128)(2,1)S(1)} %get-tuple-element.283, f32[]{:T(128)} %get-tuple-element.282, pred[256]{0:T(512)(128)(4,1)S(1)} %iota_compare_fusion.2, ...), kind=kOutput, calls=%fused_computation.8.clone.1 | convolution fusion | flops 17203200 | bytes 527880 | tf_op jit(solution)/shard_map/while/body/eval_jaxpr/jvp()/dot_general | solution.py:35
  80.0 0.7 iota_compare_fusion.2
  81.3 1.5 %fusion.105 = bf16[256,128]{1,0:T(8,128)(2,1)S(1)} fusion(f32[]{:T(128)} %get-tuple-element.285, bf16[6,256,128]{2,1,0:T(8,128)(2,1)S(1)} %get-tuple-element.284, s32[]{:T(128)S(6)} %copy.73, bf16[6,256,128]{2,1,0:T(8,128)(2,1)S(1)} %get-tuple-element.283, f32[]{:T(128)} %get-tuple-element.282, pred[256]{0:T(512)(128)(4,1)S(1)} %iota_compare_fusion.2, ...), kind=kOutput, calls=%fused_computation.8.clone.1 | convolution fusion | flops 17203200 | bytes 527880 | tf_op jit(solution)/shard_map/while/body/eval_jaxpr/jvp()/dot_general | solution.py:35
  86.7 1.5 %fusion.105 = bf16[256,128]{1,0:T(8,128)(2,1)S(1)} fusion(f32[]{:T(128)} %get-tuple-element.285, bf16[6,256,128]{2,1,0:T(8,128)(2,1)S(1)} %get-tuple-element.284, s32[]{:T(128)S(6)} %copy.73, bf16[6,256,128]{2,1,0:T(8,128)(2,1)S(1)} %get-tuple-element.283, f32[]{:T(128)} %get-tuple-element.282, pred[256]{0:T(512)(128)(4,1)S(1)} %iota_compare_fusion.2, ...), kind=kOutput, calls=%fused_computation.8.clone.1 | convolution fusion | flops 17203200 | bytes 527880 | tf_op jit(solution)/shard_map/while/body/eval_jaxpr/jvp()/dot_general | solution.py:35
  90.8 39.6 %psum.7 = f32[2,128]{1,0:T(2,128)S(1)} all-reduce(f32[2,128]{1,0:T(2,128)S(1)} %reduce_sum.78), channel_id=1, replica_groups=mesh['segment'=4,'dp'=4,'seq'=2] {'segment','dp','seq'}, use_global_device_ids=true, to_apply=%region_12.13 | all-reduce | flops 256 | bytes 2048 | tf_op jit(solution)/shard_map/psum | solution.py:109
  131.0 1.9 %copy.45 = bf16[1,256,768]{2,1,0:T(8,128)(2,1)} copy(bf16[1,256,768]{1,2,0:T(8,128)(2,1)} %bitcast.223) | data formatting | bytes 786432
  132.9 0.9 copy.46
  133.8 0.9 copy.47
  (190 shorter events, 26.1 us)
Async XLA Ops:
  0.6 1.8 %copy-start = (bf16[1,128,1536]{2,1,0:T(8,128)(2,1)S(1)}, bf16[1,128,1536]{2,1,0:T(8,128)(2,1)}, u32[]{:S(2)}) copy-start(bf16[1,128,1536]{2,1,0:T(8,128)(2,1)} %param.14) | copy-start | bytes 1179652
  1.9 3.4 %copy-start.1 = (bf16[1,128,1536]{2,1,0:T(8,128)(2,1)S(1)}, bf16[1,128,1536]{2,1,0:T(8,128)(2,1)}, u32[]{:S(2)}) copy-start(bf16[1,128,1536]{2,1,0:T(8,128)(2,1)} %param.13) | copy-start | bytes 1179652
  1.9 8.0 %collective-permute-start = (bf16[128,2,6,128]{0,3,2,1:T(8,128)(2,1)S(1)}, bf16[128,2,6,128]{0,3,2,1:T(8,128)(2,1)}, u32[]{:S(2)}, u32[]{:S(2)}) collective-permute-start(bf16[128,2,6,128]{0,3,2,1:T(8,128)(2,1)S(1)} %bitcast.227), channel_id=1, source_target_pairs={{0,8},{8,16},{16,24},{24,0},{1,9},{9,17},{17,25},{25,1},{2,10},{10... | collective-permute-start | bytes 1179656 | tf_op jit(solution)/shard_map/ppermute | solution.py:14
  2.7 11.5 %collective-permute-start.1 = (bf16[128,2,6,128]{0,3,2,1:T(8,128)(2,1)S(1)}, bf16[128,2,6,128]{0,3,2,1:T(8,128)(2,1)}, u32[]{:S(2)}, u32[]{:S(2)}) collective-permute-start(bf16[128,2,6,128]{0,3,2,1:T(8,128)(2,1)S(1)} %bitcast.226), channel_id=1, source_target_pairs={{0,8},{8,16},{16,24},{24,0},{1,9},{9,17},{17,25},{25,1},{2,10},{10... | collective-permute-start | bytes 1179656 | tf_op jit(solution)/shard_map/ppermute | solution.py:14
  5.5 20.2 %collective-permute-start.4 = (bf16[128,2,6,128]{0,3,2,1:T(8,128)(2,1)S(1)}, bf16[128,2,6,128]{0,3,2,1:T(8,128)(2,1)}, u32[]{:S(2)}, u32[]{:S(2)}) collective-permute-start(bf16[128,2,6,128]{0,3,2,1:T(8,128)(2,1)S(1)} %bitcast.225), channel_id=1, source_target_pairs={{0,8},{8,16},{16,24},{24,0},{1,9},{9,17},{17,25},{25,1},{2,10},{10... | collective-permute-start | bytes 1179656 | tf_op jit(solution)/shard_map/ppermute | solution.py:14
  9.9 10.3 %all-to-all-start = ((bf16[128,2,6,128]{0,3,2,1:T(8,128)(2,1)}), bf16[128,2,6,128]{0,3,2,1:T(8,128)(2,1)S(1)}, u32[]{:S(2)}, u32[]{:S(2)}) async-start(bf16[128,2,6,128]{0,3,2,1:T(8,128)(2,1)} %collective-permute-done), calls=%async_computation | async-start | bytes 786432 | tf_op jit(solution)/shard_map/all_to_all | solution.py:93
  13.5 10.2 %copy-start.2 = (bf16[1,128,1536]{2,1,0:T(8,128)(2,1)S(1)}, bf16[1,128,1536]{2,1,0:T(8,128)(2,1)}, u32[]{:S(2)}) copy-start(bf16[1,128,1536]{2,1,0:T(8,128)(2,1)} %param.12) | copy-start | bytes 1179652
  20.2 9.3 %all-to-all-start.1 = ((bf16[128,2,6,128]{0,3,2,1:T(8,128)(2,1)}), bf16[128,2,6,128]{0,3,2,1:T(8,128)(2,1)S(1)}, u32[]{:S(2)}, u32[]{:S(2)}) async-start(bf16[128,2,6,128]{0,3,2,1:T(8,128)(2,1)} %collective-permute-done.1), calls=%async_computation.1 | async-start | bytes 786432 | tf_op jit(solution)/shard_map/all_to_all | solution.py:92
  23.7 1.0 copy-start.3
  23.9 11.7 %collective-permute-start.3 = (bf16[128,2,6,128]{0,3,2,1:T(8,128)(2,1)S(1)}, bf16[128,2,6,128]{0,3,2,1:T(8,128)(2,1)}, u32[]{:S(2)}, u32[]{:S(2)}) collective-permute-start(bf16[128,2,6,128]{0,3,2,1:T(8,128)(2,1)S(1)} %bitcast.224), channel_id=1, source_target_pairs={{0,8},{8,16},{16,24},{24,0},{1,9},{9,17},{17,25},{25,1},{2,10},{10... | collective-permute-start | bytes 1179656 | tf_op jit(solution)/shard_map/ppermute | solution.py:14
  24.9 8.1 %copy-start.6 = (f32[16]{0:T(128)S(1)}, f32[16]{0:T(128)}, u32[]{:S(2)}) copy-start(f32[16]{0:T(128)} %param.17) | copy-start | bytes 196
  24.9 18.7 %collective-permute-start.2 = (bf16[128,2,6,128]{0,3,2,1:T(8,128)(2,1)S(1)}, bf16[128,2,6,128]{0,3,2,1:T(8,128)(2,1)}, u32[]{:S(2)}, u32[]{:S(2)}) collective-permute-start(bf16[128,2,6,128]{0,3,2,1:T(8,128)(2,1)S(1)} %bitcast.220), channel_id=1, source_target_pairs={{0,8},{8,16},{16,24},{24,0},{1,9},{9,17},{17,25},{25,1},{2,10},{10... | collective-permute-start | bytes 1179656 | tf_op jit(solution)/shard_map/ppermute | solution.py:14
  29.6 9.3 %all-to-all-start.4 = ((bf16[128,2,6,128]{0,3,2,1:T(8,128)(2,1)}), bf16[128,2,6,128]{0,3,2,1:T(8,128)(2,1)S(1)}, u32[]{:S(2)}, u32[]{:S(2)}) async-start(bf16[128,2,6,128]{0,3,2,1:T(8,128)(2,1)} %collective-permute-done.4), calls=%async_computation.4 | async-start | bytes 786432 | tf_op jit(solution)/shard_map/all_to_all | solution.py:91
  38.9 9.3 %all-to-all-start.3 = ((bf16[128,2,6,128]{0,3,2,1:T(8,128)(2,1)}), bf16[128,2,6,128]{0,3,2,1:T(8,128)(2,1)S(1)}, u32[]{:S(2)}, u32[]{:S(2)}) async-start(bf16[128,2,6,128]{0,3,2,1:T(8,128)(2,1)} %collective-permute-done.3), calls=%async_computation.3 | async-start | bytes 786432 | tf_op jit(solution)/shard_map/all_to_all | solution.py:90
  42.4 0.7 copy-start.7
  43.6 8.1 %copy-start.8 = (s32[16]{0:T(128)S(1)}, s32[16]{0:T(128)}, u32[]{:S(2)}) copy-start(s32[16]{0:T(128)} %param.18) | copy-start | bytes 196
  48.2 9.3 %all-to-all-start.2 = ((bf16[128,2,6,128]{0,3,2,1:T(8,128)(2,1)}), bf16[128,2,6,128]{0,3,2,1:T(8,128)(2,1)S(1)}, u32[]{:S(2)}, u32[]{:S(2)}) async-start(bf16[128,2,6,128]{0,3,2,1:T(8,128)(2,1)} %collective-permute-done.2), calls=%async_computation.2 | async-start | bytes 786432 | tf_op jit(solution)/shard_map/all_to_all | solution.py:89
  57.6 1.0 copy-start.4
  57.8 0.8 copy-start.5
where the time goes:
time: 135 us
  blocking collectives  39.6 us (29%)
  waiting for transfers between devices  27 us (20%)
  starting transfers between devices  21.5 us (16%)
  matrix products  17.4 us (13%)
  local copies, waits for them, and re-layouts  16.3 us (12%)
  other arithmetic  9.91 us (7%)
  between operations  2.2 us (2%)
    psum x1, blocking collectives, body(): lax.psum(jnp.sum(dg, axis=(1, 2)), ('segment', 'dp', 'seq'))  39.6 us
    dot_general x18, matrix products, forward(): return jnp.dot(weights, v_in, preferred_element_type=jnp.float32)  11.4 us
    unnamed x26, local copies, waits for them, and re-layouts  7.37 us
    all_to_all x1, waiting for transfers between devices, body(): lax.all_to_all(arrived[4], 'seq', split_axis=1, concat_axis=0, tiled=True)  6.09 us
    dot_general x18, matrix products, forward(): jnp.dot(q_rows, k_rows.T, preferred_element_type=jnp.float32)  6.04 us
    dynamic_update_slice x36, local copies, waits for them, and re-layouts, body(): dq, dk, dv, dg = lax.map(one_head, moved)  5.88 us
    ppermute x5, waiting for transfers between devices, shifted(): return lax.ppermute(value, axis, pairs)  4.94 us
    all_to_all x1, waiting for transfers between devices, body(): lax.all_to_all(arrived[1], 'seq', split_axis=1, concat_axis=0, tiled=True)  4.58 us
  transfers between devices with their start and end apart: 10, of which 7 were waited for; matrix products, arithmetic and copies ran while one was open for 4% of the time, Pallas kernels for 0%

commit v1 on v0

v1 whole, which is shorter than its diff:
```python
import functools

import jax
import jax.numpy as jnp
from jax import lax
from jax.experimental import pallas as pl
from jax.experimental.pallas import tpu as pltpu
from jax.sharding import PartitionSpec as P

HEAD = 128
STEPS = 16
GROUP = 16
AHEAD = 3
MESH = pl.DeviceIdType.MESH
F32 = jnp.float32
BF16 = jnp.bfloat16


def dot(a, b, da, db):
    return lax.dot_general(a, b, (((da,), (db,)), ((), ())), preferred_element_type=F32)


def unit_rows(x):
    wide = x.astype(F32)
    r = lax.rsqrt(jnp.mean(wide * wide, axis=-1, keepdims=True) + 1e-06)
    return wide * r, r


def unit_rows_back(grad, unit, r, gain):
    inner = grad * gain
    mean = jnp.mean(inner * unit, axis=-1, keepdims=True)
    return r * (inner - unit * mean), jnp.sum(grad * unit, axis=0, keepdims=True)


def head_grads(q_in, k_in, v, diff, gains, advantage, delta, count):
    length = q_in.shape[0]
    scale = HEAD ** -0.5
    index = lax.broadcasted_iota(jnp.int32, (length, 1), 0)
    bias = jnp.where(index < count, F32(0.0), F32(-1e30))
    row_scale = jnp.where(index < count, advantage, F32(0.0))
    q_unit, q_r = unit_rows(q_in)
    k_unit, k_r = unit_rows(k_in)
    q = (q_unit * gains[0:1]).astype(BF16)
    k = (k_unit * gains[1:2]).astype(BF16)
    raw = jnp.exp(dot(k, q, 1, 1) * scale + bias)
    soft = raw * (1.0 / jnp.sum(raw, axis=0, keepdims=True))
    weights = soft.astype(BF16)
    velocity = dot(weights, v, 0, 0)
    cotangent = (row_scale * (diff.astype(F32) + delta * velocity)).astype(BF16)
    dv = dot(weights, cotangent, 1, 0)
    dw = dot(v, cotangent, 1, 1)
    mixed = soft * dw
    ds = (mixed - soft * jnp.sum(mixed, axis=0, keepdims=True)).astype(BF16)
    dk, dg_k = unit_rows_back(dot(ds, q, 1, 0) * scale, k_unit, k_r, gains[1:2])
    dq, dg_q = unit_rows_back(dot(ds, k, 0, 0) * scale, q_unit, q_r, gains[0:1])
    return dq.astype(BF16), dk.astype(BF16), dv.astype(BF16), dg_q, dg_k


def sigma(index):
    level = 1.0 - index.astype(F32) / STEPS
    return 7.0 * level / (1.0 + 6.0 * level)


def kernel(
    sizes,
    q_ref, k_ref, v_ref, now_ref, next_ref, gains_ref, reward_ref, step_ref, count_ref,
    oq_ref, ok_ref, ov_ref, og_ref,
    qb, kb, vb, db, lat, diff, gq, gk, gv, sum1, sum2,
    lat_sem, own_sem, send_sem, recv_sem, out_send, out_recv, s1_send, s1_recv, s2_send, s2_recv,
):
    segments, replicas, shards = sizes
    seg, dp, me = (lax.axis_index(name) for name in ("segment", "dp", "seq"))
    rows, width = q_ref.shape[1], qb.shape[1]
    heads = width // HEAD

    loads = [
        pltpu.make_async_copy(ref.at[0], lat.at[i], lat_sem.at[i])
        for i, ref in enumerate((now_ref, next_ref))
    ]
    for copy in loads:
        copy.start()

    sources = (q_ref.at[0], k_ref.at[0], v_ref.at[0], diff)
    targets = (qb, kb, vb, db)
    my_rows = pl.ds(pl.multiple_of(me * rows, rows), rows)
    own_columns = pl.ds(pl.multiple_of(me * width, width), width)
    own = [
        pltpu.make_async_copy(sources[i].at[:, own_columns], targets[i].at[my_rows, :], own_sem.at[i])
        for i in range(4)
    ]
    for copy in own[:3]:
        copy.start()

    group1 = [
        (lax.rem(seg + a, segments), dp, lax.rem(me + b, shards))
        for a in range(segments)
        for b in range(shards)
        if a or b
    ]
    group2 = [(seg, lax.rem(dp + a, replicas), me) for a in range(1, replicas)]
    barrier = pltpu.get_barrier_semaphore()
    for device in group1 + group2:
        pl.semaphore_signal(barrier, inc=1, device_id=device, device_id_type=MESH)
    pl.semaphore_wait(barrier, len(group1) + len(group2))

    def part(array, head, step):
        other = lax.rem(me + step, shards)
        columns = pl.ds(pl.multiple_of(other * width + head * HEAD, HEAD), HEAD)
        return pltpu.make_async_remote_copy(
            src_ref=sources[array].at[:, columns],
            dst_ref=targets[array].at[my_rows, pl.ds(head * HEAD, HEAD)],
            send_sem=send_sem.at[array, head, step - 1],
            recv_sem=recv_sem.at[array, head, step - 1],
            device_id=(seg, dp, other),
            device_id_type=MESH,
        )

    parts = [
        [[part(i, h, s) for s in range(1, shards)] for i in range(4)] for h in range(heads)
    ]

    def send(head, arrays):
        for i in arrays:
            for copy in parts[head][i]:
                copy.start()

    ahead = min(AHEAD, heads)
    send(0, (0, 1, 2))
    for copy in loads:
        copy.wait()
    full = diff.shape[1]
    for c in range(0, full, 256):
        cols = slice(c, c + 256)
        diff[:, cols] = (lat[1, :, cols].astype(F32) - lat[0, :, cols].astype(F32)).astype(BF16)
    send(0, (3,))
    for h in range(1, ahead):
        send(h, (0, 1, 2, 3))
    own[3].start()

    video = seg * replicas + dp
    first = video // GROUP * GROUP
    one = (1, 1)
    rewards = [reward_ref[first + i] for i in range(GROUP)]
    mean = sum(rewards[1:], rewards[0]) * F32(1.0 / GROUP)
    spread = sum((r - mean) * (r - mean) for r in rewards) * F32(1.0 / GROUP)
    spread = jnp.sqrt(jnp.full(one, spread, F32))
    advantage = jnp.full(one, reward_ref[video] - mean, F32) / jnp.maximum(spread, F32(0.25))
    step = jnp.full(one, step_ref[video], jnp.int32)
    delta = sigma(step) - sigma(step + 1)
    count = count_ref[video]
    gains = gains_ref[...]

    for copy in own:
        copy.wait()

    next_device = (lax.rem(seg + 1, segments), dp, me)
    outs = []
    dg_q = jnp.zeros((1, HEAD), F32)
    dg_k = jnp.zeros((1, HEAD), F32)
    for h in range(heads):
        for i in range(4):
            for copy in parts[h][i]:
                copy.wait_recv()
        if h + ahead < heads:
            send(h + ahead, (0, 1, 2, 3))
        cols = slice(h * HEAD, (h + 1) * HEAD)
        dq, dk, dv, a, b = head_grads(
            qb[:, cols], kb[:, cols], vb[:, cols], db[:, cols], gains, advantage, delta, count
        )
        dg_q, dg_k = dg_q + a, dg_k + b
        gq[:, cols], gk[:, cols], gv[:, cols] = dq, dk, dv
        for i, (src, dst) in enumerate(((gq, oq_ref), (gk, ok_ref), (gv, ov_ref))):
            copy = pltpu.make_async_remote_copy(
                src_ref=src.at[:, cols],
                dst_ref=dst.at[0, :, cols],
                send_sem=out_send.at[i, h],
                recv_sem=out_recv.at[i, h],
                device_id=next_device,
                device_id_type=MESH,
            )
            copy.start()
            outs.append(copy)

    def spread_sum(slots, mine, value, group, sent, received):
        slots[mine] = value
        copies = [
            pltpu.make_async_remote_copy(
                src_ref=slots.at[mine],
                dst_ref=slots.at[mine],
                send_sem=sent.at[i],
                recv_sem=received.at[i],
                device_id=device,
                device_id_type=MESH,
            )
            for i, device in enumerate(group)
        ]
        for copy in copies:
            copy.start()
        for copy in copies:
            copy.wait_recv()
        total = slots[0]
        for i in range(1, len(group) + 1):
            total = total + slots[i]
        return total, copies

    share = jnp.concatenate([dg_q, dg_k, jnp.zeros((6, HEAD), F32)], axis=0)
    total, copies1 = spread_sum(sum1, seg * shards + me, share, group1, s1_send, s1_recv)
    total, copies2 = spread_sum(sum2, dp, total, group2, s2_send, s2_recv)
    og_ref[...] = total[0:2] * F32(1.0 / (segments * replicas))

    for copy in outs:
        copy.wait()
    for copy in copies1 + copies2:
        copy.wait_send()
    for head in parts:
        for array in head:
            for copy in array:
                copy.wait_send()


def body(sizes, query_in, key_in, value_in, latent_now, latent_next, gains, rewards, steps, counts):
    segments, replicas, shards = sizes
    _, rows, full = query_in.shape
    length, width = rows * shards, full // shards
    heads = width // HEAD
    any_space = pl.BlockSpec(memory_space=pltpu.HBM)
    vmem = pl.BlockSpec(memory_space=pltpu.VMEM)
    smem = pl.BlockSpec(memory_space=pltpu.SMEM)
    grad = jax.ShapeDtypeStruct((1, length, width), BF16)
    near, far = segments * shards, replicas
    dma = pltpu.SemaphoreType.DMA
    return pl.pallas_call(
        functools.partial(kernel, sizes),
        out_shape=(grad, grad, grad, jax.ShapeDtypeStruct((2, HEAD), F32)),
        in_specs=[any_space] * 5 + [vmem] + [smem] * 3,
        out_specs=(any_space, any_space, any_space, vmem),
        scratch_shapes=[pltpu.VMEM((length, width), BF16)] * 4
        + [pltpu.VMEM((2, rows, full), BF16), pltpu.VMEM((rows, full), BF16)]
        + [pltpu.VMEM((length, width), BF16)] * 3
        + [pltpu.VMEM((near, 8, HEAD), F32), pltpu.VMEM((far, 8, HEAD), F32)]
        + [dma((2,)), dma((4,))]
        + [dma((4, heads, shards - 1))] * 2
        + [dma((3, heads))] * 2
        + [dma((near - 1,))] * 2
        + [dma((far - 1,))] * 2,
        compiler_params=pltpu.CompilerParams(
            collective_id=0, has_side_effects=True, vmem_limit_bytes=63 * 1024 * 1024
        ),
        cost_estimate=pl.CostEstimate(
            flops=12 * heads * length * length * HEAD,
            bytes_accessed=16 * length * width,
            transcendentals=heads * length * length,
        ),
    )(query_in, key_in, value_in, latent_now, latent_next, gains, rewards, steps, counts)


def solution(mesh):
    sizes = tuple(mesh.shape[name] for name in ("segment", "dp", "seq"))
    rows = P(("segment", "dp"), "seq", None)
    columns = P(("segment", "dp"), None, "seq")
    return jax.shard_map(
        functools.partial(body, sizes),
        mesh=mesh,
        in_specs=(rows,) * 5 + (P(),) * 4,
        out_specs=(columns, columns, columns, P()),
        check_vma=False,
    )
```

time: 135 us -> 40.9 us (0.30)
  blocking collectives: 39.6 us -> 0 us
  Pallas kernels: 0 us -> 35.8 us
  waiting for transfers between devices: 27 us -> 0 us
  starting transfers between devices: 21.5 us -> 0 us
  matrix products: 17.4 us -> 0 us
  local copies, waits for them, and re-layouts: 16.3 us -> 4.27 us
  other arithmetic: 9.91 us -> 0 us
  between operations: 2.2 us -> 0.65 us
    psum x1 -> x0, blocking collectives: 39.6 us -> none  [body(): lax.psum(jnp.sum(dg, axis=(1, 2)), ('segment', 'dp', 'seq'))]
    pallas_call x0 -> x1, Pallas kernels: none -> 35.8 us  [body(): pl.pallas_call(functools.partial(kernel, sizes), out_shape=(grad, grad, g...]
    all_to_all x5 -> x0, waiting for transfers between devices: 22.1 us -> none  [the longest x1 6.09 us: body(): lax.all_to_all(arrived[4], 'seq', split_axis=1, concat_axis=0, tiled=True)]
    all_to_all x5 -> x0, starting transfers between devices: 17.5 us -> none  [the longest x1 3.6 us: body(): lax.all_to_all(arrived[4], 'seq', split_axis=1, concat_axis=0, tiled=True)]
    dot_general x36 -> x0, matrix products: 17.4 us -> none  [the longest x18 11.4 us: forward(): return jnp.dot(weights, v_in, preferred_element_type=jnp.float32)]
    dynamic_update_slice x36 -> x0, local copies, waits for them, and re-layouts: 5.88 us -> none  [body(): dq, dk, dv, dg = lax.map(one_head, moved)]
    ppermute x5 -> x0, waiting for transfers between devices: 4.94 us -> none  [shifted(): return lax.ppermute(value, axis, pairs)]
    ppermute x5 -> x0, starting transfers between devices: 4.08 us -> none  [shifted(): return lax.ppermute(value, axis, pairs)]
  transfers between devices with their start and end apart: 10 -> 0, of which waited for: 7 -> 0; matrix products, arithmetic and copies ran while one was open for 4% -> 0% of each run, Pallas kernels for 0% -> 0%
where the time goes in v1:
time: 40.9 us; the launch traced here: 40.7 us
  Pallas kernels  35.8 us (88%)
  local copies, waits for them, and re-layouts  4.27 us (10%)
  between operations  0.65 us (2%)
    pallas_call x1, Pallas kernels, body(): pl.pallas_call(functools.partial(kernel, sizes), out_shape=(grad, grad, g...  35.8 us
    unnamed x10, local copies, waits for them, and re-layouts  4.27 us

profile of v1, /device:TPU:0, one launch (start us, length us, event | category | flops | bytes accessed | tf_op | source)
XLA Modules:
  0.0 40.7 jit_solution(10667394640698440600)
XLA Ops:
  0.6 35.8 %shard_map.120 = (bf16[1,256,768]{2,1,0:T(8,128)(2,1)}, bf16[1,256,768]{2,1,0:T(8,128)(2,1)}, bf16[1,256,768]{2,1,0:T(8,128)(2,1)}, f32[2,128]{1,0:T(2,128)}) custom-call(bf16[1,128,1536]{2,1,0:T(8,128)(2,1)} %q_ref.1, bf16[1,128,1536]{2,1,0:T(8,128)(2,1)} %k_ref.1, bf16[1,128,1536]{2,1,0:T(8,128)(2,1)} %v_ref.1, bf16[1,128,1536]{2,1,0:T(8,128)(2,1)} %now_ref.1, ...), custom_call_target="tpu_custom_call" | custom-call | flops 603979776 | bytes 3145728 | tf_op jit(solution)/shard_map/pallas_call | solution.py:232
  36.4 0.0 copy-start.1
  36.5 1.8 %copy.17 = bf16[1,256,768]{2,1,0:T(8,128)(2,1)} copy(bf16[1,256,768]{2,1,0:T(8,128)(2,1)} %get-tuple-element.8) | data formatting | bytes 786432
  38.3 0.0 copy-done.1
  38.3 0.0 copy-start
  38.3 0.7 %copy.18 = bf16[1,256,768]{2,1,0:T(8,128)(2,1)} copy(bf16[1,256,768]{2,1,0:T(8,128)(2,1)S(1)} %copy-done.1) | data formatting | bytes 786432
  39.0 0.4 copy-done
  39.4 0.0 copy-start.2
  39.4 0.7 %copy.19 = bf16[1,256,768]{2,1,0:T(8,128)(2,1)} copy(bf16[1,256,768]{2,1,0:T(8,128)(2,1)S(1)} %copy-done) | data formatting | bytes 786432
  40.2 0.0 copy-done.2
  40.2 0.6 %copy.20 = f32[2,128]{1,0:T(2,128)} copy(f32[2,128]{1,0:T(2,128)S(1)} %copy-done.2) | data formatting | bytes 2048
Async XLA Ops:
  36.4 1.8 %copy-start.1 = (bf16[1,256,768]{2,1,0:T(8,128)(2,1)S(1)}, bf16[1,256,768]{2,1,0:T(8,128)(2,1)}, u32[]{:S(2)}) copy-start(bf16[1,256,768]{2,1,0:T(8,128)(2,1)} %get-tuple-element.9) | copy-start | bytes 1179652
  38.3 1.1 %copy-start = (bf16[1,256,768]{2,1,0:T(8,128)(2,1)S(1)}, bf16[1,256,768]{2,1,0:T(8,128)(2,1)}, u32[]{:S(2)}) copy-start(bf16[1,256,768]{2,1,0:T(8,128)(2,1)} %get-tuple-element.10) | copy-start | bytes 1179652
  39.4 0.8 %copy-start.2 = (f32[2,128]{1,0:T(2,128)S(1)}, f32[2,128]{1,0:T(2,128)}, u32[]{:S(2)}) copy-start(f32[2,128]{1,0:T(2,128)} %get-tuple-element.11) | copy-start | bytes 3076

commit v2 on v1

--- a/solution.py
+++ b/solution.py
@@ -10,7 +10,9 @@
 HEAD = 128
 STEPS = 16
 GROUP = 16
-AHEAD = 3
+AHEAD = 2
+LOG2E = 1.4426950408889634
+SCALE = HEAD ** -0.5
 MESH = pl.DeviceIdType.MESH
 F32 = jnp.float32
 BF16 = jnp.bfloat16
@@ -20,39 +22,36 @@
     return lax.dot_general(a, b, (((da,), (db,)), ((), ())), preferred_element_type=F32)
 
 
-def unit_rows(x):
+def unit_rows(x, average):
     wide = x.astype(F32)
-    r = lax.rsqrt(jnp.mean(wide * wide, axis=-1, keepdims=True) + 1e-06)
+    r = lax.rsqrt(dot((wide * wide).astype(BF16), average, 1, 0) + 1e-06)
     return wide * r, r
 
 
-def unit_rows_back(grad, unit, r, gain):
+def unit_rows_back(grad, unit, r, gain, average):
     inner = grad * gain
-    mean = jnp.mean(inner * unit, axis=-1, keepdims=True)
+    mean = dot((inner * unit).astype(BF16), average, 1, 0)
     return r * (inner - unit * mean), jnp.sum(grad * unit, axis=0, keepdims=True)
 
 
-def head_grads(q_in, k_in, v, diff, gains, advantage, delta, count):
+def head_grads(q_in, k_in, v, diff, consts, bias, row_scale, delta, average, ones):
+    q_gain, k_gain, dq_gain, dk_gain = consts
     length = q_in.shape[0]
-    scale = HEAD ** -0.5
-    index = lax.broadcasted_iota(jnp.int32, (length, 1), 0)
-    bias = jnp.where(index < count, F32(0.0), F32(-1e30))
-    row_scale = jnp.where(index < count, advantage, F32(0.0))
-    q_unit, q_r = unit_rows(q_in)
-    k_unit, k_r = unit_rows(k_in)
-    q = (q_unit * gains[0:1]).astype(BF16)
-    k = (k_unit * gains[1:2]).astype(BF16)
-    raw = jnp.exp(dot(k, q, 1, 1) * scale + bias)
-    soft = raw * (1.0 / jnp.sum(raw, axis=0, keepdims=True))
-    weights = soft.astype(BF16)
-    velocity = dot(weights, v, 0, 0)
-    cotangent = (row_scale * (diff.astype(F32) + delta * velocity)).astype(BF16)
-    dv = dot(weights, cotangent, 1, 0)
-    dw = dot(v, cotangent, 1, 1)
-    mixed = soft * dw
-    ds = (mixed - soft * jnp.sum(mixed, axis=0, keepdims=True)).astype(BF16)
-    dk, dg_k = unit_rows_back(dot(ds, q, 1, 0) * scale, k_unit, k_r, gains[1:2])
-    dq, dg_q = unit_rows_back(dot(ds, k, 0, 0) * scale, q_unit, q_r, gains[0:1])
+    q_unit, q_r = unit_rows(q_in, average)
+    k_unit, k_r = unit_rows(k_in, average)
+    q = (q_unit * q_gain).astype(BF16)
+    k = (k_unit * k_gain).astype(BF16)
+    raw = jnp.exp2(dot(q, k, 1, 1) + bias)
+    weights = raw.astype(BF16)
+    inverse = 1.0 / dot(weights, ones, 1, 0)
+    velocity = dot(weights, v, 1, 0) * inverse
+    cotangent = (row_scale * inverse * (diff.astype(F32) + delta * velocity)).astype(BF16)
+    dv = dot(weights, cotangent, 0, 0)
+    dw = dot(cotangent, v, 1, 1)
+    inner = dot((cotangent.astype(F32) * velocity).astype(BF16), ones[:HEAD], 1, 0)
+    ds = (raw * (dw - jnp.concatenate([inner] * (length // HEAD), axis=1))).astype(BF16)
+    dk, dg_k = unit_rows_back(dot(ds, q, 0, 0), k_unit, k_r, dk_gain, average)
+    dq, dg_q = unit_rows_back(dot(ds, k, 1, 0), q_unit, q_r, dq_gain, average)
     return dq.astype(BF16), dk.astype(BF16), dv.astype(BF16), dg_q, dg_k
 
 
@@ -148,7 +147,19 @@
     step = jnp.full(one, step_ref[video], jnp.int32)
     delta = sigma(step) - sigma(step + 1)
     count = count_ref[video]
-    gains = gains_ref[...]
+    q_gain, k_gain = gains_ref[0:1], gains_ref[1:2]
+    consts = (
+        q_gain * F32(SCALE * LOG2E), k_gain, q_gain * F32(SCALE), k_gain * F32(1.0 / LOG2E)
+    )
+    length = qb.shape[0]
+    average = jnp.full((HEAD, HEAD), 1.0 / HEAD, BF16)
+    ones = jnp.full((length, HEAD), 1.0, BF16)
+    bias = jnp.where(
+        lax.broadcasted_iota(jnp.int32, (1, length), 1) < count, F32(0.0), F32(-1e30)
+    )
+    row_scale = jnp.where(
+        lax.broadcasted_iota(jnp.int32, (length, HEAD), 0) < count, advantage, F32(0.0)
+    )
 
     for copy in own:
         copy.wait()
@@ -165,7 +176,8 @@
             send(h + ahead, (0, 1, 2, 3))
         cols = slice(h * HEAD, (h + 1) * HEAD)
         dq, dk, dv, a, b = head_grads(
-            qb[:, cols], kb[:, cols], vb[:, cols], db[:, cols], gains, advantage, delta, count
+            qb[:, cols], kb[:, cols], vb[:, cols], db[:, cols],
+            consts, bias, row_scale, delta, average, ones,
         )
         dg_q, dg_k = dg_q + a, dg_k + b
         gq[:, cols], gk[:, cols], gv[:, cols] = dq, dk, dv
@@ -203,7 +215,7 @@
             total = total + slots[i]
         return total, copies
 
-    share = jnp.concatenate([dg_q, dg_k, jnp.zeros((6, HEAD), F32)], axis=0)
+    share = jnp.concatenate([dg_q * F32(SCALE), dg_k * F32(1.0 / LOG2E), jnp.zeros((6, HEAD), F32)], axis=0)
     total, copies1 = spread_sum(sum1, seg * shards + me, share, group1, s1_send, s1_recv)
     total, copies2 = spread_sum(sum2, dp, total, group2, s2_send, s2_recv)
     og_ref[...] = total[0:2] * F32(1.0 / (segments * replicas))
@@ -216,6 +228,15 @@
         for array in head:
             for copy in array:
                 copy.wait_send()
+
+
+def hand_over(*refs):
+    sems = refs[8]
+    copies = [pltpu.make_async_copy(refs[i], refs[4 + i], sems.at[i]) for i in range(4)]
+    for copy in copies:
+        copy.start()
+    for copy in copies:
+        copy.wait()
 
 
 def body(sizes, query_in, key_in, value_in, latent_now, latent_next, gains, rewards, steps, counts):
@@ -229,7 +250,7 @@
     grad = jax.ShapeDtypeStruct((1, length, width), BF16)
     near, far = segments * shards, replicas
     dma = pltpu.SemaphoreType.DMA
-    return pl.pallas_call(
+    results = pl.pallas_call(
         functools.partial(kernel, sizes),
         out_shape=(grad, grad, grad, jax.ShapeDtypeStruct((2, HEAD), F32)),
         in_specs=[any_space] * 5 + [vmem] + [smem] * 3,
@@ -252,6 +273,15 @@
             transcendentals=heads * length * length,
         ),
     )(query_in, key_in, value_in, latent_now, latent_next, gains, rewards, steps, counts)
+    hbm = pl.BlockSpec(memory_space=pltpu.HBM)
+    return pl.pallas_call(
+        hand_over,
+        out_shape=(grad, grad, grad, jax.ShapeDtypeStruct((2, HEAD), F32)),
+        in_specs=[hbm] * 4,
+        out_specs=(hbm,) * 4,
+        scratch_shapes=[dma((4,))],
+        compiler_params=pltpu.CompilerParams(vmem_limit_bytes=63 * 1024 * 1024),
+    )(*results)
 
 
 def solution(mesh):

time: 40.9 us -> 73.7 us (1.80)
  Pallas kernels: 35.8 us -> 72.9 us
  local copies, waits for them, and re-layouts: 4.27 us -> 0 us
    pallas_call x0 -> x1, Pallas kernels: none -> 36.9 us  [body(): pl.pallas_call(hand_over, out_shape=(grad, grad, grad, jax.ShapeDtypeStru...]
    unnamed x10 -> x0, local copies, waits for them, and re-layouts: 4.27 us -> none
where the time goes in v2:
time: 73.7 us; the launch traced here: 73.5 us
  Pallas kernels  72.9 us (99%)
    pallas_call x1, Pallas kernels, body(): pl.pallas_call(hand_over, out_shape=(grad, grad, grad, jax.ShapeDtypeStru...  36.9 us
    pallas_call x1, Pallas kernels, body(): pl.pallas_call(functools.partial(kernel, sizes), out_shape=(grad, grad, g...  36 us

profile of v2, /device:TPU:0, one launch (start us, length us, event | category | flops | bytes accessed | tf_op | source)
XLA Modules:
  0.0 73.5 jit_solution(15714277361190971162)
XLA Ops:
  0.6 36.0 %shard_map.120 = (bf16[1,256,768]{2,1,0:T(8,128)(2,1)}, bf16[1,256,768]{2,1,0:T(8,128)(2,1)}, bf16[1,256,768]{2,1,0:T(8,128)(2,1)}, f32[2,128]{1,0:T(2,128)}) custom-call(bf16[1,128,1536]{2,1,0:T(8,128)(2,1)} %q_ref.1, bf16[1,128,1536]{2,1,0:T(8,128)(2,1)} %k_ref.1, bf16[1,128,1536]{2,1,0:T(8,128)(2,1)} %v_ref.1, bf16[1,128,1536]{2,1,0:T(8,128)(2,1)} %now_ref.1, ...), custom_call_target="tpu_custom_call" | custom-call | flops 603979776 | bytes 3145728 | tf_op jit(solution)/shard_map/pallas_call | solution.py:253
  36.6 36.9 %shard_map.121 = (bf16[1,256,768]{2,1,0:T(8,128)(2,1)}, bf16[1,256,768]{2,1,0:T(8,128)(2,1)}, bf16[1,256,768]{2,1,0:T(8,128)(2,1)}, f32[2,128]{1,0:T(2,128)}) custom-call(bf16[1,256,768]{2,1,0:T(8,128)(2,1)} %get-tuple-element.8.refs_0_, bf16[1,256,768]{2,1,0:T(8,128)(2,1)} %get-tuple-element.9.refs_1_, bf16[1,256,768]{2,1,0:T(8,128)(2,1)} %get-tuple-element.10.refs_2_, ...), custom_call_target="tpu_custom_call" | custom-call | tf_op jit(solution)/shard_map/pallas_call | solution.py:277

commit v3 on v2

--- a/solution.py
+++ b/solution.py
@@ -64,8 +64,8 @@
     sizes,
     q_ref, k_ref, v_ref, now_ref, next_ref, gains_ref, reward_ref, step_ref, count_ref,
     oq_ref, ok_ref, ov_ref, og_ref,
-    qb, kb, vb, db, lat, diff, gq, gk, gv, sum1, sum2,
-    lat_sem, own_sem, send_sem, recv_sem, out_send, out_recv, s1_send, s1_recv, s2_send, s2_recv,
+    qs, ks, vs, qb, kb, vb, db, lat, diff, gq, gk, gv, rq, rk, rv, sum1, sum2,
+    load_sem, store_sem, send_sem, recv_sem, out_send, out_recv, s1_send, s1_recv, s2_send, s2_recv,
 ):
     segments, replicas, shards = sizes
     seg, dp, me = (lax.axis_index(name) for name in ("segment", "dp", "seq"))
@@ -73,22 +73,18 @@
     heads = width // HEAD
 
     loads = [
-        pltpu.make_async_copy(ref.at[0], lat.at[i], lat_sem.at[i])
-        for i, ref in enumerate((now_ref, next_ref))
+        pltpu.make_async_copy(ref.at[0], dst, load_sem.at[i])
+        for i, (ref, dst) in enumerate(
+            ((q_ref, qs), (k_ref, ks), (v_ref, vs), (now_ref, lat.at[0]), (next_ref, lat.at[1]))
+        )
     ]
     for copy in loads:
         copy.start()
 
-    sources = (q_ref.at[0], k_ref.at[0], v_ref.at[0], diff)
+    sources = (qs, ks, vs, diff)
     targets = (qb, kb, vb, db)
     my_rows = pl.ds(pl.multiple_of(me * rows, rows), rows)
     own_columns = pl.ds(pl.multiple_of(me * width, width), width)
-    own = [
-        pltpu.make_async_copy(sources[i].at[:, own_columns], targets[i].at[my_rows, :], own_sem.at[i])
-        for i in range(4)
-    ]
-    for copy in own[:3]:
-        copy.start()
 
     group1 = [
         (lax.rem(seg + a, segments), dp, lax.rem(me + b, shards))
@@ -124,8 +120,10 @@
                 copy.start()
 
     ahead = min(AHEAD, heads)
-    send(0, (0, 1, 2))
-    for copy in loads:
+    for i in range(3):
+        loads[i].wait()
+        send(0, (i,))
+    for copy in loads[3:]:
         copy.wait()
     full = diff.shape[1]
     for c in range(0, full, 256):
@@ -134,7 +132,8 @@
     send(0, (3,))
     for h in range(1, ahead):
         send(h, (0, 1, 2, 3))
-    own[3].start()
+    for source, target in zip(sources, targets):
+        target[my_rows, :] = source[:, own_columns]
 
     video = seg * replicas + dp
     first = video // GROUP * GROUP
@@ -161,13 +160,21 @@
         lax.broadcasted_iota(jnp.int32, (length, HEAD), 0) < count, advantage, F32(0.0)
     )
 
-    for copy in own:
-        copy.wait()
-
     next_device = (lax.rem(seg + 1, segments), dp, me)
-    outs = []
+    outs, stores = [], []
     dg_q = jnp.zeros((1, HEAD), F32)
     dg_k = jnp.zeros((1, HEAD), F32)
+
+    def store(head):
+        cols = slice(head * HEAD, (head + 1) * HEAD)
+        for i, (src, dst) in enumerate(((rq, oq_ref), (rk, ok_ref), (rv, ov_ref))):
+            outs[head][i].wait_recv()
+            copy = pltpu.make_async_copy(
+                src.at[:, cols], dst.at[0, :, cols], store_sem.at[i, head]
+            )
+            copy.start()
+            stores.append(copy)
+
     for h in range(heads):
         for i in range(4):
             for copy in parts[h][i]:
@@ -181,17 +188,21 @@
         )
         dg_q, dg_k = dg_q + a, dg_k + b
         gq[:, cols], gk[:, cols], gv[:, cols] = dq, dk, dv
-        for i, (src, dst) in enumerate(((gq, oq_ref), (gk, ok_ref), (gv, ov_ref))):
+        head_outs = []
+        for i, (src, dst) in enumerate(((gq, rq), (gk, rk), (gv, rv))):
             copy = pltpu.make_async_remote_copy(
                 src_ref=src.at[:, cols],
-                dst_ref=dst.at[0, :, cols],
+                dst_ref=dst.at[:, cols],
                 send_sem=out_send.at[i, h],
                 recv_sem=out_recv.at[i, h],
                 device_id=next_device,
                 device_id_type=MESH,
             )
             copy.start()
-            outs.append(copy)
+            head_outs.append(copy)
+        outs.append(head_outs)
+        if h >= 1:
+            store(h - 1)
 
     def spread_sum(slots, mine, value, group, sent, received):
         slots[mine] = value
@@ -220,7 +231,11 @@
     total, copies2 = spread_sum(sum2, dp, total, group2, s2_send, s2_recv)
     og_ref[...] = total[0:2] * F32(1.0 / (segments * replicas))
 
-    for copy in outs:
+    store(heads - 1)
+    for head in outs:
+        for copy in head:
+            copy.wait_send()
+    for copy in stores:
         copy.wait()
     for copy in copies1 + copies2:
         copy.wait_send()
@@ -230,13 +245,29 @@
                 copy.wait_send()
 
 
-def hand_over(*refs):
-    sems = refs[8]
-    copies = [pltpu.make_async_copy(refs[i], refs[4 + i], sems.at[i]) for i in range(4)]
-    for copy in copies:
-        copy.start()
-    for copy in copies:
-        copy.wait()
+def hand_over(pieces, *refs):
+    ins, outs, holds, sums, in_sem, out_sem = refs[:4], refs[4:8], refs[8:11], refs[11], refs[12], refs[13]
+    rows = ins[0].shape[1] // pieces
+    todo = []
+    for p in range(pieces):
+        part = pl.ds(p * rows, rows)
+        for i in range(3):
+            hold = holds[i].at[part]
+            todo.append((
+                pltpu.make_async_copy(ins[i].at[0, part], hold, in_sem.at[i, p]),
+                pltpu.make_async_copy(hold, outs[i].at[0, part], out_sem.at[i, p]),
+            ))
+    todo.append((
+        pltpu.make_async_copy(ins[3], sums, in_sem.at[3, 0]),
+        pltpu.make_async_copy(sums, outs[3], out_sem.at[3, 0]),
+    ))
+    for load, _ in todo:
+        load.start()
+    for load, store in todo:
+        load.wait()
+        store.start()
+    for _, store in todo:
+        store.wait()
 
 
 def body(sizes, query_in, key_in, value_in, latent_now, latent_next, gains, rewards, steps, counts):
@@ -255,11 +286,12 @@
         out_shape=(grad, grad, grad, jax.ShapeDtypeStruct((2, HEAD), F32)),
         in_specs=[any_space] * 5 + [vmem] + [smem] * 3,
         out_specs=(any_space, any_space, any_space, vmem),
-        scratch_shapes=[pltpu.VMEM((length, width), BF16)] * 4
+        scratch_shapes=[pltpu.VMEM((rows, full), BF16)] * 3
+        + [pltpu.VMEM((length, width), BF16)] * 4
         + [pltpu.VMEM((2, rows, full), BF16), pltpu.VMEM((rows, full), BF16)]
-        + [pltpu.VMEM((length, width), BF16)] * 3
+        + [pltpu.VMEM((length, width), BF16)] * 6
         + [pltpu.VMEM((near, 8, HEAD), F32), pltpu.VMEM((far, 8, HEAD), F32)]
-        + [dma((2,)), dma((4,))]
+        + [dma((5,)), dma((3, heads))]
         + [dma((4, heads, shards - 1))] * 2
         + [dma((3, heads))] * 2
         + [dma((near - 1,))] * 2
@@ -275,11 +307,12 @@
     )(query_in, key_in, value_in, latent_now, latent_next, gains, rewards, steps, counts)
     hbm = pl.BlockSpec(memory_space=pltpu.HBM)
     return pl.pallas_call(
-        hand_over,
+        functools.partial(hand_over, 2),
         out_shape=(grad, grad, grad, jax.ShapeDtypeStruct((2, HEAD), F32)),
         in_specs=[hbm] * 4,
         out_specs=(hbm,) * 4,
-        scratch_shapes=[dma((4,))],
+        scratch_shapes=[pltpu.VMEM((length, width), BF16)] * 3
+        + [pltpu.VMEM((2, HEAD), F32), dma((4, 2)), dma((4, 2))],
         compiler_params=pltpu.CompilerParams(vmem_limit_bytes=63 * 1024 * 1024),
     )(*results)
 

time: 73.7 us -> 39.5 us (0.54)
  Pallas kernels: 72.9 us -> 38.7 us
    pallas_call x1, Pallas kernels: 36.9 us -> 2.17 us  [body(): pl.pallas_call(functools.partial(hand_over, 2), out_shape=(grad, grad, gr...]
where the time goes in v3:
time: 39.5 us; the launch traced here: 39.3 us
  Pallas kernels  38.7 us (98%)
  between operations  0.64 us (2%)
    pallas_call x1, Pallas kernels, body(): pl.pallas_call(functools.partial(kernel, sizes), out_shape=(grad, grad, g...  36.5 us
    pallas_call x1, Pallas kernels, body(): pl.pallas_call(functools.partial(hand_over, 2), out_shape=(grad, grad, gr...  2.17 us

profile of v3, /device:TPU:0, one launch (start us, length us, event | category | flops | bytes accessed | tf_op | source)
XLA Modules:
  0.0 39.3 jit_solution(9604549424124248232)
XLA Ops:
  0.6 36.5 %shard_map.120 = (bf16[1,256,768]{2,1,0:T(8,128)(2,1)}, bf16[1,256,768]{2,1,0:T(8,128)(2,1)}, bf16[1,256,768]{2,1,0:T(8,128)(2,1)}, f32[2,128]{1,0:T(2,128)}) custom-call(bf16[1,128,1536]{2,1,0:T(8,128)(2,1)} %q_ref.1, bf16[1,128,1536]{2,1,0:T(8,128)(2,1)} %k_ref.1, bf16[1,128,1536]{2,1,0:T(8,128)(2,1)} %v_ref.1, bf16[1,128,1536]{2,1,0:T(8,128)(2,1)} %now_ref.1, ...), custom_call_target="tpu_custom_call" | custom-call | flops 603979776 | bytes 3145728 | tf_op jit(solution)/shard_map/pallas_call | solution.py:284
  37.1 2.2 %shard_map.121 = (bf16[1,256,768]{2,1,0:T(8,128)(2,1)}, bf16[1,256,768]{2,1,0:T(8,128)(2,1)}, bf16[1,256,768]{2,1,0:T(8,128)(2,1)}, f32[2,128]{1,0:T(2,128)}) custom-call(bf16[1,256,768]{2,1,0:T(8,128)(2,1)} %get-tuple-element.8.refs_0_, bf16[1,256,768]{2,1,0:T(8,128)(2,1)} %get-tuple-element.9.refs_1_, bf16[1,256,768]{2,1,0:T(8,128)(2,1)} %get-tuple-element.10.refs_2_, ...), custom_call_target="tpu_custom_call" | custom-call | tf_op jit(solution)/shard_map/pallas_call | solution.py:309

commit v4 on v3

--- a/solution.py
+++ b/solution.py
@@ -69,8 +69,8 @@
 ):
     segments, replicas, shards = sizes
     seg, dp, me = (lax.axis_index(name) for name in ("segment", "dp", "seq"))
-    rows, width = q_ref.shape[1], qb.shape[1]
-    heads = width // HEAD
+    rows, heads = q_ref.shape[1], qb.shape[0]
+    width = heads * HEAD
 
     loads = [
         pltpu.make_async_copy(ref.at[0], dst, load_sem.at[i])
@@ -84,7 +84,6 @@
     sources = (qs, ks, vs, diff)
     targets = (qb, kb, vb, db)
     my_rows = pl.ds(pl.multiple_of(me * rows, rows), rows)
-    own_columns = pl.ds(pl.multiple_of(me * width, width), width)
 
     group1 = [
         (lax.rem(seg + a, segments), dp, lax.rem(me + b, shards))
@@ -103,21 +102,19 @@
         columns = pl.ds(pl.multiple_of(other * width + head * HEAD, HEAD), HEAD)
         return pltpu.make_async_remote_copy(
             src_ref=sources[array].at[:, columns],
-            dst_ref=targets[array].at[my_rows, pl.ds(head * HEAD, HEAD)],
+            dst_ref=targets[array].at[head, my_rows],
             send_sem=send_sem.at[array, head, step - 1],
             recv_sem=recv_sem.at[array, head, step - 1],
             device_id=(seg, dp, other),
             device_id_type=MESH,
         )
 
-    parts = [
-        [[part(i, h, s) for s in range(1, shards)] for i in range(4)] for h in range(heads)
-    ]
-
-    def send(head, arrays):
-        for i in arrays:
-            for copy in parts[head][i]:
-                copy.start()
+    def parts(head, arrays=(0, 1, 2, 3)):
+        return [part(i, head, s) for i in arrays for s in range(1, shards)]
+
+    def send(head, arrays=(0, 1, 2, 3)):
+        for copy in parts(head, arrays):
+            copy.start()
 
     ahead = min(AHEAD, heads)
     for i in range(3):
@@ -131,9 +128,7 @@
         diff[:, cols] = (lat[1, :, cols].astype(F32) - lat[0, :, cols].astype(F32)).astype(BF16)
     send(0, (3,))
     for h in range(1, ahead):
-        send(h, (0, 1, 2, 3))
-    for source, target in zip(sources, targets):
-        target[my_rows, :] = source[:, own_columns]
+        send(h)
 
     video = seg * replicas + dp
     first = video // GROUP * GROUP
@@ -150,7 +145,7 @@
     consts = (
         q_gain * F32(SCALE * LOG2E), k_gain, q_gain * F32(SCALE), k_gain * F32(1.0 / LOG2E)
     )
-    length = qb.shape[0]
+    length = qb.shape[1]
     average = jnp.full((HEAD, HEAD), 1.0 / HEAD, BF16)
     ones = jnp.full((length, HEAD), 1.0, BF16)
     bias = jnp.where(
@@ -161,48 +156,59 @@
     )
 
     next_device = (lax.rem(seg + 1, segments), dp, me)
-    outs, stores = [], []
-    dg_q = jnp.zeros((1, HEAD), F32)
-    dg_k = jnp.zeros((1, HEAD), F32)
-
-    def store(head):
-        cols = slice(head * HEAD, (head + 1) * HEAD)
-        for i, (src, dst) in enumerate(((rq, oq_ref), (rk, ok_ref), (rv, ov_ref))):
-            outs[head][i].wait_recv()
-            copy = pltpu.make_async_copy(
-                src.at[:, cols], dst.at[0, :, cols], store_sem.at[i, head]
-            )
-            copy.start()
-            stores.append(copy)
-
-    for h in range(heads):
-        for i in range(4):
-            for copy in parts[h][i]:
-                copy.wait_recv()
-        if h + ahead < heads:
-            send(h + ahead, (0, 1, 2, 3))
-        cols = slice(h * HEAD, (h + 1) * HEAD)
-        dq, dk, dv, a, b = head_grads(
-            qb[:, cols], kb[:, cols], vb[:, cols], db[:, cols],
-            consts, bias, row_scale, delta, average, ones,
-        )
-        dg_q, dg_k = dg_q + a, dg_k + b
-        gq[:, cols], gk[:, cols], gv[:, cols] = dq, dk, dv
-        head_outs = []
-        for i, (src, dst) in enumerate(((gq, rq), (gk, rk), (gv, rv))):
-            copy = pltpu.make_async_remote_copy(
-                src_ref=src.at[:, cols],
-                dst_ref=dst.at[:, cols],
-                send_sem=out_send.at[i, h],
-                recv_sem=out_recv.at[i, h],
+    grads = ((gq, rq, oq_ref), (gk, rk, ok_ref), (gv, rv, ov_ref))
+
+    def outs(head):
+        return [
+            pltpu.make_async_remote_copy(
+                src_ref=src.at[head],
+                dst_ref=dst.at[head],
+                send_sem=out_send.at[i, head],
+                recv_sem=out_recv.at[i, head],
                 device_id=next_device,
                 device_id_type=MESH,
             )
+            for i, (src, dst, _) in enumerate(grads)
+        ]
+
+    def stores(head):
+        cols = pl.ds(pl.multiple_of(head * HEAD, HEAD), HEAD)
+        return [
+            pltpu.make_async_copy(src.at[head], dst.at[0, :, cols], store_sem.at[i, head])
+            for i, (_, src, dst) in enumerate(grads)
+        ]
+
+    def store(head):
+        for copy, onward in zip(outs(head), stores(head)):
+            copy.wait_recv()
+            onward.start()
+
+    def one_head(h, sums):
+        own = pl.ds(pl.multiple_of(me * width + h * HEAD, HEAD), HEAD)
+        for source, target in zip(sources, targets):
+            target[h, my_rows] = source[:, own]
+        for copy in parts(h):
+            copy.wait_recv()
+
+        @pl.when(h + ahead < heads)
+        def _():
+            send(h + ahead)
+
+        dq, dk, dv, dg_q, dg_k = head_grads(
+            qb[h], kb[h], vb[h], db[h], consts, bias, row_scale, delta, average, ones
+        )
+        gq[h], gk[h], gv[h] = dq, dk, dv
+        for copy in outs(h):
             copy.start()
-            head_outs.append(copy)
-        outs.append(head_outs)
-        if h >= 1:
+
+        @pl.when(h >= 1)
+        def _():
             store(h - 1)
+
+        return sums[0] + dg_q, sums[1] + dg_k
+
+    zero = jnp.zeros((1, HEAD), F32)
+    dg_q, dg_k = lax.fori_loop(0, heads, one_head, (zero, zero))
 
     def spread_sum(slots, mine, value, group, sent, received):
         slots[mine] = value
@@ -232,17 +238,15 @@
     og_ref[...] = total[0:2] * F32(1.0 / (segments * replicas))
 
     store(heads - 1)
-    for head in outs:
-        for copy in head:
-            copy.wait_send()
-    for copy in stores:
-        copy.wait()
     for copy in copies1 + copies2:
         copy.wait_send()
-    for head in parts:
-        for array in head:
-            for copy in array:
-                copy.wait_send()
+
+    @pl.loop(0, heads)
+    def _(h):
+        for copy in outs(h) + parts(h):
+            copy.wait_send()
+        for copy in stores(h):
+            copy.wait()
 
 
 def hand_over(pieces, *refs):
@@ -287,9 +291,9 @@
         in_specs=[any_space] * 5 + [vmem] + [smem] * 3,
         out_specs=(any_space, any_space, any_space, vmem),
         scratch_shapes=[pltpu.VMEM((rows, full), BF16)] * 3
-        + [pltpu.VMEM((length, width), BF16)] * 4
+        + [pltpu.VMEM((heads, length, HEAD), BF16)] * 4
         + [pltpu.VMEM((2, rows, full), BF16), pltpu.VMEM((rows, full), BF16)]
-        + [pltpu.VMEM((length, width), BF16)] * 6
+        + [pltpu.VMEM((heads, length, HEAD), BF16)] * 6
         + [pltpu.VMEM((near, 8, HEAD), F32), pltpu.VMEM((far, 8, HEAD), F32)]
         + [dma((5,)), dma((3, heads))]
         + [dma((4, heads, shards - 1))] * 2

time: 39.5 us -> 39.4 us (level)
  no operation moved by 1% of the time
where the time goes in v4:
time: 39.4 us; the launch traced here: 39.3 us
  Pallas kernels  38.6 us (98%)
  between operations  0.64 us (2%)
    pallas_call x1, Pallas kernels, body(): pl.pallas_call(functools.partial(kernel, sizes), out_shape=(grad, grad, g...  36.4 us
    pallas_call x1, Pallas kernels, body(): pl.pallas_call(functools.partial(hand_over, 2), out_shape=(grad, grad, gr...  2.17 us

profile of v4, /device:TPU:0, one launch (start us, length us, event | category | flops | bytes accessed | tf_op | source)
XLA Modules:
  0.0 39.3 jit_solution(14148985204686045736)
XLA Ops:
  0.6 36.4 %shard_map.120 = (bf16[1,256,768]{2,1,0:T(8,128)(2,1)}, bf16[1,256,768]{2,1,0:T(8,128)(2,1)}, bf16[1,256,768]{2,1,0:T(8,128)(2,1)}, f32[2,128]{1,0:T(2,128)}) custom-call(bf16[1,128,1536]{2,1,0:T(8,128)(2,1)} %q_ref.1, bf16[1,128,1536]{2,1,0:T(8,128)(2,1)} %k_ref.1, bf16[1,128,1536]{2,1,0:T(8,128)(2,1)} %v_ref.1, bf16[1,128,1536]{2,1,0:T(8,128)(2,1)} %now_ref.1, ...), custom_call_target="tpu_custom_call" | custom-call | flops 603979776 | bytes 3145728 | tf_op jit(solution)/shard_map/pallas_call | solution.py:288
  37.1 2.2 %shard_map.121 = (bf16[1,256,768]{2,1,0:T(8,128)(2,1)}, bf16[1,256,768]{2,1,0:T(8,128)(2,1)}, bf16[1,256,768]{2,1,0:T(8,128)(2,1)}, f32[2,128]{1,0:T(2,128)}) custom-call(bf16[1,256,768]{2,1,0:T(8,128)(2,1)} %get-tuple-element.8.refs_0_, bf16[1,256,768]{2,1,0:T(8,128)(2,1)} %get-tuple-element.9.refs_1_, bf16[1,256,768]{2,1,0:T(8,128)(2,1)} %get-tuple-element.10.refs_2_, ...), custom_call_target="tpu_custom_call" | custom-call | tf_op jit(solution)/shard_map/pallas_call | solution.py:313

commit v5 on v4

--- a/solution.py
+++ b/solution.py
@@ -22,37 +22,14 @@
     return lax.dot_general(a, b, (((da,), (db,)), ((), ())), preferred_element_type=F32)
 
 
-def unit_rows(x, average):
-    wide = x.astype(F32)
-    r = lax.rsqrt(dot((wide * wide).astype(BF16), average, 1, 0) + 1e-06)
-    return wide * r, r
+def inverse_rms(wide, average):
+    return lax.rsqrt(dot((wide * wide).astype(BF16), average, 1, 0) + 1e-06)
 
 
 def unit_rows_back(grad, unit, r, gain, average):
     inner = grad * gain
     mean = dot((inner * unit).astype(BF16), average, 1, 0)
     return r * (inner - unit * mean), jnp.sum(grad * unit, axis=0, keepdims=True)
-
-
-def head_grads(q_in, k_in, v, diff, consts, bias, row_scale, delta, average, ones):
-    q_gain, k_gain, dq_gain, dk_gain = consts
-    length = q_in.shape[0]
-    q_unit, q_r = unit_rows(q_in, average)
-    k_unit, k_r = unit_rows(k_in, average)
-    q = (q_unit * q_gain).astype(BF16)
-    k = (k_unit * k_gain).astype(BF16)
-    raw = jnp.exp2(dot(q, k, 1, 1) + bias)
-    weights = raw.astype(BF16)
-    inverse = 1.0 / dot(weights, ones, 1, 0)
-    velocity = dot(weights, v, 1, 0) * inverse
-    cotangent = (row_scale * inverse * (diff.astype(F32) + delta * velocity)).astype(BF16)
-    dv = dot(weights, cotangent, 0, 0)
-    dw = dot(cotangent, v, 1, 1)
-    inner = dot((cotangent.astype(F32) * velocity).astype(BF16), ones[:HEAD], 1, 0)
-    ds = (raw * (dw - jnp.concatenate([inner] * (length // HEAD), axis=1))).astype(BF16)
-    dk, dg_k = unit_rows_back(dot(ds, q, 0, 0), k_unit, k_r, dk_gain, average)
-    dq, dg_q = unit_rows_back(dot(ds, k, 1, 0), q_unit, q_r, dq_gain, average)
-    return dq.astype(BF16), dk.astype(BF16), dv.astype(BF16), dg_q, dg_k
 
 
 def sigma(index):
@@ -116,19 +93,27 @@
         for copy in parts(head, arrays):
             copy.start()
 
-    ahead = min(AHEAD, heads)
+    together = next(n for n in (2, 1) if heads % n == 0)
+    groups = heads // together
+    ahead = min(AHEAD, groups)
+
+    def send_group(g, arrays=(0, 1, 2, 3)):
+        for i in arrays:
+            for j in range(together):
+                send(g * together + j, (i,))
+
     for i in range(3):
         loads[i].wait()
-        send(0, (i,))
+        send_group(0, (i,))
     for copy in loads[3:]:
         copy.wait()
     full = diff.shape[1]
     for c in range(0, full, 256):
         cols = slice(c, c + 256)
         diff[:, cols] = (lat[1, :, cols].astype(F32) - lat[0, :, cols].astype(F32)).astype(BF16)
-    send(0, (3,))
-    for h in range(1, ahead):
-        send(h)
+    send_group(0, (3,))
+    for g in range(1, ahead):
+        send_group(g)
 
     video = seg * replicas + dp
     first = video // GROUP * GROUP
@@ -142,18 +127,17 @@
     delta = sigma(step) - sigma(step + 1)
     count = count_ref[video]
     q_gain, k_gain = gains_ref[0:1], gains_ref[1:2]
-    consts = (
-        q_gain * F32(SCALE * LOG2E), k_gain, q_gain * F32(SCALE), k_gain * F32(1.0 / LOG2E)
-    )
+    q_gain_log2 = q_gain * F32(SCALE * LOG2E)
+    dq_gain, dk_gain = q_gain * F32(SCALE), k_gain * F32(1.0 / LOG2E)
     length = qb.shape[1]
     average = jnp.full((HEAD, HEAD), 1.0 / HEAD, BF16)
     ones = jnp.full((length, HEAD), 1.0, BF16)
-    bias = jnp.where(
-        lax.broadcasted_iota(jnp.int32, (1, length), 1) < count, F32(0.0), F32(-1e30)
-    )
-    row_scale = jnp.where(
-        lax.broadcasted_iota(jnp.int32, (length, HEAD), 0) < count, advantage, F32(0.0)
-    )
+    valid = lax.broadcasted_iota(jnp.int32, (length, HEAD), 0) < count
+    row_scale = jnp.where(valid, advantage, F32(0.0))
+    valid_ones = jnp.where(valid, F32(1.0), F32(0.0)).astype(BF16)
+
+    def wide_lanes(x):
+        return jnp.concatenate([x] * (length // HEAD), axis=1)
 
     next_device = (lax.rem(seg + 1, segments), dp, me)
     grads = ((gq, rq, oq_ref), (gk, rk, ok_ref), (gv, rv, ov_ref))
@@ -183,32 +167,81 @@
             copy.wait_recv()
             onward.start()
 
-    def one_head(h, sums):
-        own = pl.ds(pl.multiple_of(me * width + h * HEAD, HEAD), HEAD)
-        for source, target in zip(sources, targets):
-            target[h, my_rows] = source[:, own]
-        for copy in parts(h):
-            copy.wait_recv()
-
-        @pl.when(h + ahead < heads)
+    def wait(hs, array):
+        for h in hs:
+            for copy in parts(h, (array,)):
+                copy.wait_recv()
+
+    def one_group(g, sums):
+        hs = [g * together + j for j in range(together)]
+        for h in hs:
+            own = pl.ds(pl.multiple_of(me * width + h * HEAD, HEAD), HEAD)
+            for source, target in zip(sources, targets):
+                target[h, my_rows] = source[:, own]
+        wait(hs, 0)
+
+        @pl.when(g + ahead < groups)
         def _():
-            send(h + ahead)
-
-        dq, dk, dv, dg_q, dg_k = head_grads(
-            qb[h], kb[h], vb[h], db[h], consts, bias, row_scale, delta, average, ones
-        )
-        gq[h], gk[h], gv[h] = dq, dk, dv
-        for copy in outs(h):
-            copy.start()
-
-        @pl.when(h >= 1)
+            send_group(g + ahead)
+
+        wait(hs, 1)
+        q_wide = [qb[h].astype(F32) for h in hs]
+        k_wide = [kb[h].astype(F32) for h in hs]
+        q_r = [inverse_rms(x, average) for x in q_wide]
+        k_r = [jnp.where(valid, inverse_rms(x, average), F32(0.0)) for x in k_wide]
+        q_unit = [x * r for x, r in zip(q_wide, q_r)]
+        k_unit = [x * r for x, r in zip(k_wide, k_r)]
+        q = [(x * q_gain_log2).astype(BF16) for x in q_unit]
+        k = [(x * k_gain).astype(BF16) for x in k_unit]
+        raw = [jnp.exp2(dot(a, b, 1, 1)) for a, b in zip(q, k)]
+        weights = [x.astype(BF16) for x in raw]
+        inverse = [1.0 / dot(x, valid_ones, 1, 0) for x in weights]
+        raw_by_key = [jnp.exp2(dot(a, b, 1, 1)) for a, b in zip(k, q)]
+        weights_by_key = [x.astype(BF16) for x in raw_by_key]
+        wait(hs, 2)
+        v = [vb[h] * valid_ones for h in hs]
+        velocity = [dot(x, y, 1, 0) * z for x, y, z in zip(weights, v, inverse)]
+        wait(hs, 3)
+        cotangent = [
+            (row_scale * z * (db[h].astype(F32) + delta * x)).astype(BF16)
+            for h, x, z in zip(hs, velocity, inverse)
+        ]
+        for h, x, y in zip(hs, weights_by_key, cotangent):
+            gv[h] = jnp.where(valid, dot(x, y, 1, 0), F32(0.0)).astype(BF16)
+        along = [(x.astype(F32) * y).astype(BF16) for x, y in zip(cotangent, velocity)]
+        inner = [dot(x, ones[:HEAD], 1, 0) for x in along]
+        inner_by_key = [dot(ones, x, 1, 1) for x in along]
+        ds_by_key = [
+            (z * (dot(x, y, 1, 1) - i)).astype(BF16)
+            for x, y, z, i in zip(v, cotangent, raw_by_key, inner_by_key)
+        ]
+        ds = [
+            (z * (dot(y, x, 1, 1) - wide_lanes(i))).astype(BF16)
+            for x, y, z, i in zip(v, cotangent, raw, inner)
+        ]
+        dk = [
+            unit_rows_back(dot(x, y, 1, 0), u, r, dk_gain, average)
+            for x, y, u, r in zip(ds_by_key, q, k_unit, k_r)
+        ]
+        dq = [
+            unit_rows_back(dot(x, y, 1, 0), u, r, dq_gain, average)
+            for x, y, u, r in zip(ds, k, q_unit, q_r)
+        ]
+        for h, x, y in zip(hs, dq, dk):
+            gq[h], gk[h] = x[0].astype(BF16), y[0].astype(BF16)
+        for h in hs:
+            for copy in outs(h):
+                copy.start()
+
+        @pl.when(g >= 1)
         def _():
-            store(h - 1)
-
-        return sums[0] + dg_q, sums[1] + dg_k
+            for h in hs:
+                store(h - together)
+
+        return sum((x[1] for x in dq), sums[0]), sum((x[1] for x in dk), sums[1])
 
     zero = jnp.zeros((1, HEAD), F32)
-    dg_q, dg_k = lax.fori_loop(0, heads, one_head, (zero, zero))
+    dg_q, dg_k = lax.fori_loop(0, groups, one_group, (zero, zero))
 
     def spread_sum(slots, mine, value, group, sent, received):
         slots[mine] = value
@@ -237,7 +270,8 @@
     total, copies2 = spread_sum(sum2, dp, total, group2, s2_send, s2_recv)
     og_ref[...] = total[0:2] * F32(1.0 / (segments * replicas))
 
-    store(heads - 1)
+    for h in range(heads - together, heads):
+        store(h)
     for copy in copies1 + copies2:
         copy.wait_send()
 

time: 39.4 us -> 41.5 us (1.053)
  Pallas kernels: 38.6 us -> 40.7 us
    pallas_call x1, Pallas kernels: 36.4 us -> 38.6 us  [body(): pl.pallas_call(functools.partial(kernel, sizes), out_shape=(grad, grad, g...]
where the time goes in v5:
time: 41.5 us; the launch traced here: 41.4 us
  Pallas kernels  40.7 us (98%)
  between operations  0.64 us (2%)
    pallas_call x1, Pallas kernels, body(): pl.pallas_call(functools.partial(kernel, sizes), out_shape=(grad, grad, g...  38.6 us
    pallas_call x1, Pallas kernels, body(): pl.pallas_call(functools.partial(hand_over, 2), out_shape=(grad, grad, gr...  2.17 us

profile of v5, /device:TPU:0, one launch (start us, length us, event | category | flops | bytes accessed | tf_op | source)
XLA Modules:
  0.0 41.4 jit_solution(4339280977551551509)
XLA Ops:
  0.6 38.6 %shard_map.120 = (bf16[1,256,768]{2,1,0:T(8,128)(2,1)}, bf16[1,256,768]{2,1,0:T(8,128)(2,1)}, bf16[1,256,768]{2,1,0:T(8,128)(2,1)}, f32[2,128]{1,0:T(2,128)}) custom-call(bf16[1,128,1536]{2,1,0:T(8,128)(2,1)} %q_ref.1, bf16[1,128,1536]{2,1,0:T(8,128)(2,1)} %k_ref.1, bf16[1,128,1536]{2,1,0:T(8,128)(2,1)} %v_ref.1, bf16[1,128,1536]{2,1,0:T(8,128)(2,1)} %now_ref.1, ...), custom_call_target="tpu_custom_call" | custom-call | flops 603979776 | bytes 3145728 | tf_op jit(solution)/shard_map/pallas_call | solution.py:322
  39.2 2.2 %shard_map.121 = (bf16[1,256,768]{2,1,0:T(8,128)(2,1)}, bf16[1,256,768]{2,1,0:T(8,128)(2,1)}, bf16[1,256,768]{2,1,0:T(8,128)(2,1)}, f32[2,128]{1,0:T(2,128)}) custom-call(bf16[1,256,768]{2,1,0:T(8,128)(2,1)} %get-tuple-element.8.refs_0_, bf16[1,256,768]{2,1,0:T(8,128)(2,1)} %get-tuple-element.9.refs_1_, bf16[1,256,768]{2,1,0:T(8,128)(2,1)} %get-tuple-element.10.refs_2_, ...), custom_call_target="tpu_custom_call" | custom-call | tf_op jit(solution)/shard_map/pallas_call | solution.py:347

commit v6 on v5

--- a/solution.py
+++ b/solution.py
@@ -10,7 +10,7 @@
 HEAD = 128
 STEPS = 16
 GROUP = 16
-AHEAD = 2
+AHEAD = 3
 LOG2E = 1.4426950408889634
 SCALE = HEAD ** -0.5
 MESH = pl.DeviceIdType.MESH
@@ -41,8 +41,8 @@
     sizes,
     q_ref, k_ref, v_ref, now_ref, next_ref, gains_ref, reward_ref, step_ref, count_ref,
     oq_ref, ok_ref, ov_ref, og_ref,
-    qs, ks, vs, qb, kb, vb, db, lat, diff, gq, gk, gv, rq, rk, rv, sum1, sum2,
-    load_sem, store_sem, send_sem, recv_sem, out_send, out_recv, s1_send, s1_recv, s2_send, s2_recv,
+    qs, ks, vs, qb, kb, vb, db, lat, diff, gq, gk, gv, sum1, sum2,
+    load_sem, store_sem, send_sem, recv_sem, s1_send, s1_recv, s2_send, s2_recv,
 ):
     segments, replicas, shards = sizes
     seg, dp, me = (lax.axis_index(name) for name in ("segment", "dp", "seq"))
@@ -80,20 +80,20 @@
         return pltpu.make_async_remote_copy(
             src_ref=sources[array].at[:, columns],
             dst_ref=targets[array].at[head, my_rows],
-            send_sem=send_sem.at[array, head, step - 1],
-            recv_sem=recv_sem.at[array, head, step - 1],
-            device_id=(seg, dp, other),
+            send_sem=send_sem.at[array, head, step],
+            recv_sem=recv_sem.at[array, head, step],
+            device_id=(lax.rem(seg + 1, segments), dp, other),
             device_id_type=MESH,
         )
 
     def parts(head, arrays=(0, 1, 2, 3)):
-        return [part(i, head, s) for i in arrays for s in range(1, shards)]
+        return [part(i, head, s) for i in arrays for s in range(shards)]
 
     def send(head, arrays=(0, 1, 2, 3)):
         for copy in parts(head, arrays):
             copy.start()
 
-    together = next(n for n in (2, 1) if heads % n == 0)
+    together = next(n for n in (1,) if heads % n == 0)
     groups = heads // together
     ahead = min(AHEAD, groups)
 
@@ -115,7 +115,7 @@
     for g in range(1, ahead):
         send_group(g)
 
-    video = seg * replicas + dp
+    video = lax.rem(seg + segments - 1, segments) * replicas + dp
     first = video // GROUP * GROUP
     one = (1, 1)
     rewards = [reward_ref[first + i] for i in range(GROUP)]
@@ -139,33 +139,12 @@
     def wide_lanes(x):
         return jnp.concatenate([x] * (length // HEAD), axis=1)
 
-    next_device = (lax.rem(seg + 1, segments), dp, me)
-    grads = ((gq, rq, oq_ref), (gk, rk, ok_ref), (gv, rv, ov_ref))
-
-    def outs(head):
-        return [
-            pltpu.make_async_remote_copy(
-                src_ref=src.at[head],
-                dst_ref=dst.at[head],
-                send_sem=out_send.at[i, head],
-                recv_sem=out_recv.at[i, head],
-                device_id=next_device,
-                device_id_type=MESH,
-            )
-            for i, (src, dst, _) in enumerate(grads)
-        ]
-
     def stores(head):
         cols = pl.ds(pl.multiple_of(head * HEAD, HEAD), HEAD)
         return [
             pltpu.make_async_copy(src.at[head], dst.at[0, :, cols], store_sem.at[i, head])
-            for i, (_, src, dst) in enumerate(grads)
-        ]
-
-    def store(head):
-        for copy, onward in zip(outs(head), stores(head)):
-            copy.wait_recv()
-            onward.start()
+            for i, (src, dst) in enumerate(((gq, oq_ref), (gk, ok_ref), (gv, ov_ref)))
+        ]
 
     def wait(hs, array):
         for h in hs:
@@ -174,10 +153,6 @@
 
     def one_group(g, sums):
         hs = [g * together + j for j in range(together)]
-        for h in hs:
-            own = pl.ds(pl.multiple_of(me * width + h * HEAD, HEAD), HEAD)
-            for source, target in zip(sources, targets):
-                target[h, my_rows] = source[:, own]
         wait(hs, 0)
 
         @pl.when(g + ahead < groups)
@@ -230,14 +205,8 @@
         for h, x, y in zip(hs, dq, dk):
             gq[h], gk[h] = x[0].astype(BF16), y[0].astype(BF16)
         for h in hs:
-            for copy in outs(h):
+            for copy in stores(h):
                 copy.start()
-
-        @pl.when(g >= 1)
-        def _():
-            for h in hs:
-                store(h - together)
-
         return sum((x[1] for x in dq), sums[0]), sum((x[1] for x in dk), sums[1])
 
     zero = jnp.zeros((1, HEAD), F32)
@@ -270,14 +239,12 @@
     total, copies2 = spread_sum(sum2, dp, total, group2, s2_send, s2_recv)
     og_ref[...] = total[0:2] * F32(1.0 / (segments * replicas))
 
-    for h in range(heads - together, heads):
-        store(h)
     for copy in copies1 + copies2:
         copy.wait_send()
 
     @pl.loop(0, heads)
     def _(h):
-        for copy in outs(h) + parts(h):
+        for copy in parts(h):
             copy.wait_send()
         for copy in stores(h):
             copy.wait()
@@ -327,11 +294,10 @@
         scratch_shapes=[pltpu.VMEM((rows, full), BF16)] * 3
         + [pltpu.VMEM((heads, length, HEAD), BF16)] * 4
         + [pltpu.VMEM((2, rows, full), BF16), pltpu.VMEM((rows, full), BF16)]
-        + [pltpu.VMEM((heads, length, HEAD), BF16)] * 6
+        + [pltpu.VMEM((heads, length, HEAD), BF16)] * 3
         + [pltpu.VMEM((near, 8, HEAD), F32), pltpu.VMEM((far, 8, HEAD), F32)]
         + [dma((5,)), dma((3, heads))]
-        + [dma((4, heads, shards - 1))] * 2
-        + [dma((3, heads))] * 2
+        + [dma((4, heads, shards))] * 2
         + [dma((near - 1,))] * 2
         + [dma((far - 1,))] * 2,
         compiler_params=pltpu.CompilerParams(

time: 41.5 us -> 37.9 us (0.913)
  Pallas kernels: 40.7 us -> 37.1 us
    pallas_call x1, Pallas kernels: 38.6 us -> 35 us  [body(): pl.pallas_call(functools.partial(kernel, sizes), out_shape=(grad, grad, g...]
where the time goes in v6:
time: 37.9 us; the launch traced here: 37.8 us
  Pallas kernels  37.1 us (98%)
  between operations  0.64 us (2%)
    pallas_call x1, Pallas kernels, body(): pl.pallas_call(functools.partial(kernel, sizes), out_shape=(grad, grad, g...  35 us
    pallas_call x1, Pallas kernels, body(): pl.pallas_call(functools.partial(hand_over, 2), out_shape=(grad, grad, gr...  2.17 us

profile of v6, /device:TPU:0, one launch (start us, length us, event | category | flops | bytes accessed | tf_op | source)
XLA Modules:
  0.0 37.8 jit_solution(5851606609085147398)
XLA Ops:
  0.6 35.0 %shard_map.120 = (bf16[1,256,768]{2,1,0:T(8,128)(2,1)}, bf16[1,256,768]{2,1,0:T(8,128)(2,1)}, bf16[1,256,768]{2,1,0:T(8,128)(2,1)}, f32[2,128]{1,0:T(2,128)}) custom-call(bf16[1,128,1536]{2,1,0:T(8,128)(2,1)} %q_ref.1, bf16[1,128,1536]{2,1,0:T(8,128)(2,1)} %k_ref.1, bf16[1,128,1536]{2,1,0:T(8,128)(2,1)} %v_ref.1, bf16[1,128,1536]{2,1,0:T(8,128)(2,1)} %now_ref.1, ...), custom_call_target="tpu_custom_call" | custom-call | flops 603979776 | bytes 3145728 | tf_op jit(solution)/shard_map/pallas_call | solution.py:289
  35.6 2.2 %shard_map.121 = (bf16[1,256,768]{2,1,0:T(8,128)(2,1)}, bf16[1,256,768]{2,1,0:T(8,128)(2,1)}, bf16[1,256,768]{2,1,0:T(8,128)(2,1)}, f32[2,128]{1,0:T(2,128)}) custom-call(bf16[1,256,768]{2,1,0:T(8,128)(2,1)} %get-tuple-element.8.refs_0_, bf16[1,256,768]{2,1,0:T(8,128)(2,1)} %get-tuple-element.9.refs_1_, bf16[1,256,768]{2,1,0:T(8,128)(2,1)} %get-tuple-element.10.refs_2_, ...), custom_call_target="tpu_custom_call" | custom-call | tf_op jit(solution)/shard_map/pallas_call | solution.py:313

commit v7 on v6

--- a/solution.py
+++ b/solution.py
@@ -41,12 +41,12 @@
     sizes,
     q_ref, k_ref, v_ref, now_ref, next_ref, gains_ref, reward_ref, step_ref, count_ref,
     oq_ref, ok_ref, ov_ref, og_ref,
-    qs, ks, vs, qb, kb, vb, db, lat, diff, gq, gk, gv, sum1, sum2,
+    qs, ks, vs, lat, ready, held, gq, gk, gv, sum1, sum2,
     load_sem, store_sem, send_sem, recv_sem, s1_send, s1_recv, s2_send, s2_recv,
 ):
     segments, replicas, shards = sizes
     seg, dp, me = (lax.axis_index(name) for name in ("segment", "dp", "seq"))
-    rows, heads = q_ref.shape[1], qb.shape[0]
+    rows, heads = q_ref.shape[1], held.shape[1]
     width = heads * HEAD
 
     loads = [
@@ -58,8 +58,6 @@
     for copy in loads:
         copy.start()
 
-    sources = (qs, ks, vs, diff)
-    targets = (qb, kb, vb, db)
     my_rows = pl.ds(pl.multiple_of(me * rows, rows), rows)
 
     group1 = [
@@ -72,48 +70,43 @@
     barrier = pltpu.get_barrier_semaphore()
     for device in group1 + group2:
         pl.semaphore_signal(barrier, inc=1, device_id=device, device_id_type=MESH)
+
+    for i, ref in enumerate((qs, ks, vs)):
+        loads[i].wait()
+        for h in range(heads * shards):
+            ready[i // 2, h, i % 2] = ref[:, h * HEAD : (h + 1) * HEAD]
+    for copy in loads[3:]:
+        copy.wait()
+    for h in range(heads * shards):
+        cols = slice(h * HEAD, (h + 1) * HEAD)
+        change = lat[1, :, cols].astype(F32) - lat[0, :, cols].astype(F32)
+        ready[1, h, 1] = change.astype(BF16)
     pl.semaphore_wait(barrier, len(group1) + len(group2))
 
-    def part(array, head, step):
-        other = lax.rem(me + step, shards)
-        columns = pl.ds(pl.multiple_of(other * width + head * HEAD, HEAD), HEAD)
-        return pltpu.make_async_remote_copy(
-            src_ref=sources[array].at[:, columns],
-            dst_ref=targets[array].at[head, my_rows],
-            send_sem=send_sem.at[array, head, step],
-            recv_sem=recv_sem.at[array, head, step],
-            device_id=(lax.rem(seg + 1, segments), dp, other),
-            device_id_type=MESH,
-        )
-
-    def parts(head, arrays=(0, 1, 2, 3)):
-        return [part(i, head, s) for i in arrays for s in range(shards)]
-
-    def send(head, arrays=(0, 1, 2, 3)):
-        for copy in parts(head, arrays):
+    def parts(head, pairs=(0, 1)):
+        copies = []
+        for pair in pairs:
+            for step in range(shards):
+                other = lax.rem(me + step, shards)
+                copies.append(pltpu.make_async_remote_copy(
+                    src_ref=ready.at[pair, other * heads + head],
+                    dst_ref=held.at[pair, head, :, my_rows],
+                    send_sem=send_sem.at[pair, head, step],
+                    recv_sem=recv_sem.at[pair, head, step],
+                    device_id=(lax.rem(seg + 1, segments), dp, other),
+                    device_id_type=MESH,
+                ))
+        return copies
+
+    def send(head):
+        for copy in parts(head):
             copy.start()
 
-    together = next(n for n in (1,) if heads % n == 0)
+    together = 1
     groups = heads // together
     ahead = min(AHEAD, groups)
-
-    def send_group(g, arrays=(0, 1, 2, 3)):
-        for i in arrays:
-            for j in range(together):
-                send(g * together + j, (i,))
-
-    for i in range(3):
-        loads[i].wait()
-        send_group(0, (i,))
-    for copy in loads[3:]:
-        copy.wait()
-    full = diff.shape[1]
-    for c in range(0, full, 256):
-        cols = slice(c, c + 256)
-        diff[:, cols] = (lat[1, :, cols].astype(F32) - lat[0, :, cols].astype(F32)).astype(BF16)
-    send_group(0, (3,))
-    for g in range(1, ahead):
-        send_group(g)
+    for h in range(ahead):
+        send(h)
 
     video = lax.rem(seg + segments - 1, segments) * replicas + dp
     first = video // GROUP * GROUP
@@ -129,7 +122,7 @@
     q_gain, k_gain = gains_ref[0:1], gains_ref[1:2]
     q_gain_log2 = q_gain * F32(SCALE * LOG2E)
     dq_gain, dk_gain = q_gain * F32(SCALE), k_gain * F32(1.0 / LOG2E)
-    length = qb.shape[1]
+    length = held.shape[3]
     average = jnp.full((HEAD, HEAD), 1.0 / HEAD, BF16)
     ones = jnp.full((length, HEAD), 1.0, BF16)
     valid = lax.broadcasted_iota(jnp.int32, (length, HEAD), 0) < count
@@ -146,9 +139,9 @@
             for i, (src, dst) in enumerate(((gq, oq_ref), (gk, ok_ref), (gv, ov_ref)))
         ]
 
-    def wait(hs, array):
+    def wait(hs, pair):
         for h in hs:
-            for copy in parts(h, (array,)):
+            for copy in parts(h, (pair,)):
                 copy.wait_recv()
 
     def one_group(g, sums):
@@ -157,11 +150,10 @@
 
         @pl.when(g + ahead < groups)
         def _():
-            send_group(g + ahead)
-
-        wait(hs, 1)
-        q_wide = [qb[h].astype(F32) for h in hs]
-        k_wide = [kb[h].astype(F32) for h in hs]
+            send(g + ahead)
+
+        q_wide = [held[0, h, 0].astype(F32) for h in hs]
+        k_wide = [held[0, h, 1].astype(F32) for h in hs]
         q_r = [inverse_rms(x, average) for x in q_wide]
         k_r = [jnp.where(valid, inverse_rms(x, average), F32(0.0)) for x in k_wide]
         q_unit = [x * r for x, r in zip(q_wide, q_r)]
@@ -173,12 +165,11 @@
         inverse = [1.0 / dot(x, valid_ones, 1, 0) for x in weights]
         raw_by_key = [jnp.exp2(dot(a, b, 1, 1)) for a, b in zip(k, q)]
         weights_by_key = [x.astype(BF16) for x in raw_by_key]
-        wait(hs, 2)
-        v = [vb[h] * valid_ones for h in hs]
+        wait(hs, 1)
+        v = [held[1, h, 0] * valid_ones for h in hs]
         velocity = [dot(x, y, 1, 0) * z for x, y, z in zip(weights, v, inverse)]
-        wait(hs, 3)
         cotangent = [
-            (row_scale * z * (db[h].astype(F32) + delta * x)).astype(BF16)
+            (row_scale * z * (held[1, h, 1].astype(F32) + delta * x)).astype(BF16)
             for h, x, z in zip(hs, velocity, inverse)
         ]
         for h, x, y in zip(hs, weights_by_key, cotangent):
@@ -292,12 +283,12 @@
         in_specs=[any_space] * 5 + [vmem] + [smem] * 3,
         out_specs=(any_space, any_space, any_space, vmem),
         scratch_shapes=[pltpu.VMEM((rows, full), BF16)] * 3
-        + [pltpu.VMEM((heads, length, HEAD), BF16)] * 4
-        + [pltpu.VMEM((2, rows, full), BF16), pltpu.VMEM((rows, full), BF16)]
+        + [pltpu.VMEM((2, rows, full), BF16), pltpu.VMEM((2, full // HEAD, 2, rows, HEAD), BF16)]
+        + [pltpu.VMEM((2, heads, 2, length, HEAD), BF16)]
         + [pltpu.VMEM((heads, length, HEAD), BF16)] * 3
         + [pltpu.VMEM((near, 8, HEAD), F32), pltpu.VMEM((far, 8, HEAD), F32)]
         + [dma((5,)), dma((3, heads))]
-        + [dma((4, heads, shards))] * 2
+        + [dma((2, heads, shards))] * 2
         + [dma((near - 1,))] * 2
         + [dma((far - 1,))] * 2,
         compiler_params=pltpu.CompilerParams(

time: 37.9 us -> 37.7 us (level)
  no operation moved by 1% of the time
where the time goes in v7:
time: 37.7 us; the launch traced here: 37.5 us
  Pallas kernels  36.8 us (98%)
  between operations  0.64 us (2%)
    pallas_call x1, Pallas kernels, body(): pl.pallas_call(functools.partial(kernel, sizes), out_shape=(grad, grad, g...  34.7 us
    pallas_call x1, Pallas kernels, body(): pl.pallas_call(functools.partial(hand_over, 2), out_shape=(grad, grad, gr...  2.17 us

profile of v7, /device:TPU:0, one launch (start us, length us, event | category | flops | bytes accessed | tf_op | source)
XLA Modules:
  0.0 37.5 jit_solution(5015376867293678098)
XLA Ops:
  0.6 34.7 %shard_map.120 = (bf16[1,256,768]{2,1,0:T(8,128)(2,1)}, bf16[1,256,768]{2,1,0:T(8,128)(2,1)}, bf16[1,256,768]{2,1,0:T(8,128)(2,1)}, f32[2,128]{1,0:T(2,128)}) custom-call(bf16[1,128,1536]{2,1,0:T(8,128)(2,1)} %q_ref.1, bf16[1,128,1536]{2,1,0:T(8,128)(2,1)} %k_ref.1, bf16[1,128,1536]{2,1,0:T(8,128)(2,1)} %v_ref.1, bf16[1,128,1536]{2,1,0:T(8,128)(2,1)} %now_ref.1, ...), custom_call_target="tpu_custom_call" | custom-call | flops 603979776 | bytes 3145728 | tf_op jit(solution)/shard_map/pallas_call | solution.py:280
  35.3 2.2 %shard_map.121 = (bf16[1,256,768]{2,1,0:T(8,128)(2,1)}, bf16[1,256,768]{2,1,0:T(8,128)(2,1)}, bf16[1,256,768]{2,1,0:T(8,128)(2,1)}, f32[2,128]{1,0:T(2,128)}) custom-call(bf16[1,256,768]{2,1,0:T(8,128)(2,1)} %get-tuple-element.8.refs_0_, bf16[1,256,768]{2,1,0:T(8,128)(2,1)} %get-tuple-element.9.refs_1_, bf16[1,256,768]{2,1,0:T(8,128)(2,1)} %get-tuple-element.10.refs_2_, ...), custom_call_target="tpu_custom_call" | custom-call | tf_op jit(solution)/shard_map/pallas_call | solution.py:304

commit v8 on v7

--- a/solution.py
+++ b/solution.py
@@ -10,7 +10,7 @@
 HEAD = 128
 STEPS = 16
 GROUP = 16
-AHEAD = 3
+AHEAD = 6
 LOG2E = 1.4426950408889634
 SCALE = HEAD ** -0.5
 MESH = pl.DeviceIdType.MESH
@@ -22,13 +22,13 @@
     return lax.dot_general(a, b, (((da,), (db,)), ((), ())), preferred_element_type=F32)
 
 
-def inverse_rms(wide, average):
-    return lax.rsqrt(dot((wide * wide).astype(BF16), average, 1, 0) + 1e-06)
-
-
-def unit_rows_back(grad, unit, r, gain, average):
+def inverse_rms(wide):
+    return lax.rsqrt(jnp.mean(wide * wide, axis=-1, keepdims=True) + 1e-06)
+
+
+def unit_rows_back(grad, unit, r, gain):
     inner = grad * gain
-    mean = dot((inner * unit).astype(BF16), average, 1, 0)
+    mean = jnp.mean(inner * unit, axis=-1, keepdims=True)
     return r * (inner - unit * mean), jnp.sum(grad * unit, axis=0, keepdims=True)
 
 
@@ -123,14 +123,14 @@
     q_gain_log2 = q_gain * F32(SCALE * LOG2E)
     dq_gain, dk_gain = q_gain * F32(SCALE), k_gain * F32(1.0 / LOG2E)
     length = held.shape[3]
-    average = jnp.full((HEAD, HEAD), 1.0 / HEAD, BF16)
-    ones = jnp.full((length, HEAD), 1.0, BF16)
     valid = lax.broadcasted_iota(jnp.int32, (length, HEAD), 0) < count
+    valid_column = lax.broadcasted_iota(jnp.int32, (length, 1), 0) < count
     row_scale = jnp.where(valid, advantage, F32(0.0))
     valid_ones = jnp.where(valid, F32(1.0), F32(0.0)).astype(BF16)
-
-    def wide_lanes(x):
-        return jnp.concatenate([x] * (length // HEAD), axis=1)
+    minus_ones = jnp.full((length, HEAD), -1.0, BF16)
+
+    def beside(x, y):
+        return jnp.concatenate([x, y], axis=1)
 
     def stores(head):
         cols = pl.ds(pl.multiple_of(head * HEAD, HEAD), HEAD)
@@ -154,44 +154,42 @@
 
         q_wide = [held[0, h, 0].astype(F32) for h in hs]
         k_wide = [held[0, h, 1].astype(F32) for h in hs]
-        q_r = [inverse_rms(x, average) for x in q_wide]
-        k_r = [jnp.where(valid, inverse_rms(x, average), F32(0.0)) for x in k_wide]
+        q_r = [inverse_rms(x) for x in q_wide]
+        k_r = [jnp.where(valid_column, inverse_rms(x), F32(0.0)) for x in k_wide]
         q_unit = [x * r for x, r in zip(q_wide, q_r)]
         k_unit = [x * r for x, r in zip(k_wide, k_r)]
         q = [(x * q_gain_log2).astype(BF16) for x in q_unit]
         k = [(x * k_gain).astype(BF16) for x in k_unit]
         raw = [jnp.exp2(dot(a, b, 1, 1)) for a, b in zip(q, k)]
         weights = [x.astype(BF16) for x in raw]
-        inverse = [1.0 / dot(x, valid_ones, 1, 0) for x in weights]
         raw_by_key = [jnp.exp2(dot(a, b, 1, 1)) for a, b in zip(k, q)]
         weights_by_key = [x.astype(BF16) for x in raw_by_key]
         wait(hs, 1)
         v = [held[1, h, 0] * valid_ones for h in hs]
-        velocity = [dot(x, y, 1, 0) * z for x, y, z in zip(weights, v, inverse)]
+        summed = [dot(x, beside(y, valid_ones), 1, 0) for x, y in zip(weights, v)]
+        inverse = [1.0 / x[:, HEAD:] for x in summed]
+        velocity = [x[:, :HEAD] * y for x, y in zip(summed, inverse)]
         cotangent = [
             (row_scale * z * (held[1, h, 1].astype(F32) + delta * x)).astype(BF16)
             for h, x, z in zip(hs, velocity, inverse)
         ]
         for h, x, y in zip(hs, weights_by_key, cotangent):
             gv[h] = jnp.where(valid, dot(x, y, 1, 0), F32(0.0)).astype(BF16)
-        along = [(x.astype(F32) * y).astype(BF16) for x, y in zip(cotangent, velocity)]
-        inner = [dot(x, ones[:HEAD], 1, 0) for x in along]
-        inner_by_key = [dot(ones, x, 1, 1) for x in along]
+        left = [
+            beside(x, (x.astype(F32) * y).astype(BF16)) for x, y in zip(cotangent, velocity)
+        ]
+        right = [beside(x, minus_ones) for x in v]
+        ds = [(z * dot(x, y, 1, 1)).astype(BF16) for x, y, z in zip(left, right, raw)]
         ds_by_key = [
-            (z * (dot(x, y, 1, 1) - i)).astype(BF16)
-            for x, y, z, i in zip(v, cotangent, raw_by_key, inner_by_key)
-        ]
-        ds = [
-            (z * (dot(y, x, 1, 1) - wide_lanes(i))).astype(BF16)
-            for x, y, z, i in zip(v, cotangent, raw, inner)
+            (z * dot(y, x, 1, 1)).astype(BF16) for x, y, z in zip(left, right, raw_by_key)
+        ]
+        dq = [
+            unit_rows_back(dot(x, y, 1, 0), u, r, dq_gain)
+            for x, y, u, r in zip(ds, k, q_unit, q_r)
         ]
         dk = [
-            unit_rows_back(dot(x, y, 1, 0), u, r, dk_gain, average)
+            unit_rows_back(dot(x, y, 1, 0), u, r, dk_gain)
             for x, y, u, r in zip(ds_by_key, q, k_unit, k_r)
-        ]
-        dq = [
-            unit_rows_back(dot(x, y, 1, 0), u, r, dq_gain, average)
-            for x, y, u, r in zip(ds, k, q_unit, q_r)
         ]
         for h, x, y in zip(hs, dq, dk):
             gq[h], gk[h] = x[0].astype(BF16), y[0].astype(BF16)

time: 37.7 us -> 37.6 us (level)
  no operation moved by 1% of the time
where the time goes in v8:
time: 37.6 us; the launch traced here: 37.4 us
  Pallas kernels  36.7 us (98%)
  between operations  0.64 us (2%)
    pallas_call x1, Pallas kernels, body(): pl.pallas_call(functools.partial(kernel, sizes), out_shape=(grad, grad, g...  34.6 us
    pallas_call x1, Pallas kernels, body(): pl.pallas_call(functools.partial(hand_over, 2), out_shape=(grad, grad, gr...  2.17 us

profile of v8, /device:TPU:0, one launch (start us, length us, event | category | flops | bytes accessed | tf_op | source)
XLA Modules:
  0.0 37.4 jit_solution(8440194626667928221)
XLA Ops:
  0.6 34.6 %shard_map.120 = (bf16[1,256,768]{2,1,0:T(8,128)(2,1)}, bf16[1,256,768]{2,1,0:T(8,128)(2,1)}, bf16[1,256,768]{2,1,0:T(8,128)(2,1)}, f32[2,128]{1,0:T(2,128)}) custom-call(bf16[1,128,1536]{2,1,0:T(8,128)(2,1)} %q_ref.1, bf16[1,128,1536]{2,1,0:T(8,128)(2,1)} %k_ref.1, bf16[1,128,1536]{2,1,0:T(8,128)(2,1)} %v_ref.1, bf16[1,128,1536]{2,1,0:T(8,128)(2,1)} %now_ref.1, ...), custom_call_target="tpu_custom_call" | custom-call | flops 603979776 | bytes 3145728 | tf_op jit(solution)/shard_map/pallas_call | solution.py:278
  35.2 2.2 %shard_map.121 = (bf16[1,256,768]{2,1,0:T(8,128)(2,1)}, bf16[1,256,768]{2,1,0:T(8,128)(2,1)}, bf16[1,256,768]{2,1,0:T(8,128)(2,1)}, f32[2,128]{1,0:T(2,128)}) custom-call(bf16[1,256,768]{2,1,0:T(8,128)(2,1)} %get-tuple-element.8.refs_0_, bf16[1,256,768]{2,1,0:T(8,128)(2,1)} %get-tuple-element.9.refs_1_, bf16[1,256,768]{2,1,0:T(8,128)(2,1)} %get-tuple-element.10.refs_2_, ...), custom_call_target="tpu_custom_call" | custom-call | tf_op jit(solution)/shard_map/pallas_call | solution.py:302

commit v9 on v8

--- a/solution.py
+++ b/solution.py
@@ -86,7 +86,7 @@
     def parts(head, pairs=(0, 1)):
         copies = []
         for pair in pairs:
-            for step in range(shards):
+            for step in reversed(range(shards)):
                 other = lax.rem(me + step, shards)
                 copies.append(pltpu.make_async_remote_copy(
                     src_ref=ready.at[pair, other * heads + head],
@@ -300,12 +300,12 @@
     )(query_in, key_in, value_in, latent_now, latent_next, gains, rewards, steps, counts)
     hbm = pl.BlockSpec(memory_space=pltpu.HBM)
     return pl.pallas_call(
-        functools.partial(hand_over, 2),
+        functools.partial(hand_over, 4),
         out_shape=(grad, grad, grad, jax.ShapeDtypeStruct((2, HEAD), F32)),
         in_specs=[hbm] * 4,
         out_specs=(hbm,) * 4,
         scratch_shapes=[pltpu.VMEM((length, width), BF16)] * 3
-        + [pltpu.VMEM((2, HEAD), F32), dma((4, 2)), dma((4, 2))],
+        + [pltpu.VMEM((2, HEAD), F32), dma((4, 4)), dma((4, 4))],
         compiler_params=pltpu.CompilerParams(vmem_limit_bytes=63 * 1024 * 1024),
     )(*results)
 

time: 37.6 us -> 37.1 us (0.987)
  Pallas kernels: 36.7 us -> 36.3 us
    pallas_call x1, Pallas kernels: 34.6 us -> 34 us  [body(): pl.pallas_call(functools.partial(kernel, sizes), out_shape=(grad, grad, g...]
where the time goes in v9:
time: 37.1 us; the launch traced here: 36.9 us
  Pallas kernels  36.3 us (98%)
  between operations  0.64 us (2%)
    pallas_call x1, Pallas kernels, body(): pl.pallas_call(functools.partial(kernel, sizes), out_shape=(grad, grad, g...  34 us
    pallas_call x1, Pallas kernels, body(): pl.pallas_call(functools.partial(hand_over, 4), out_shape=(grad, grad, gr...  2.27 us

profile of v9, /device:TPU:0, one launch (start us, length us, event | category | flops | bytes accessed | tf_op | source)
XLA Modules:
  0.0 36.9 jit_solution(6588816715651065336)
XLA Ops:
  0.6 34.0 %shard_map.120 = (bf16[1,256,768]{2,1,0:T(8,128)(2,1)}, bf16[1,256,768]{2,1,0:T(8,128)(2,1)}, bf16[1,256,768]{2,1,0:T(8,128)(2,1)}, f32[2,128]{1,0:T(2,128)}) custom-call(bf16[1,128,1536]{2,1,0:T(8,128)(2,1)} %q_ref.1, bf16[1,128,1536]{2,1,0:T(8,128)(2,1)} %k_ref.1, bf16[1,128,1536]{2,1,0:T(8,128)(2,1)} %v_ref.1, bf16[1,128,1536]{2,1,0:T(8,128)(2,1)} %now_ref.1, ...), custom_call_target="tpu_custom_call" | custom-call | flops 603979776 | bytes 3145728 | tf_op jit(solution)/shard_map/pallas_call | solution.py:278
  34.6 2.3 %shard_map.121 = (bf16[1,256,768]{2,1,0:T(8,128)(2,1)}, bf16[1,256,768]{2,1,0:T(8,128)(2,1)}, bf16[1,256,768]{2,1,0:T(8,128)(2,1)}, f32[2,128]{1,0:T(2,128)}) custom-call(bf16[1,256,768]{2,1,0:T(8,128)(2,1)} %get-tuple-element.8.refs_0_, bf16[1,256,768]{2,1,0:T(8,128)(2,1)} %get-tuple-element.9.refs_1_, bf16[1,256,768]{2,1,0:T(8,128)(2,1)} %get-tuple-element.10.refs_2_, ...), custom_call_target="tpu_custom_call" | custom-call | tf_op jit(solution)/shard_map/pallas_call | solution.py:302
